TPU v7x, 128 devices: a whole 4x4x4 slice. The times are simulated.
128 devices in a mesh: dp: 16 (over z, x), seq: 8 (over y, core).
Axes of the slice: x: 4, y: 4, z: 4, core: 2. Of those that a mesh axis runs over, the one named last changes fastest.
Arguments:
- features: bfloat16 [16, 4096, 512], P('dp', 'seq'), may hold values from -16 to 16
- input_weight: bfloat16 [512, 1536], replicated, may hold values from -1 to 1
- output_weight: bfloat16 [512, 512], replicated, may hold values from -0.25 to 0.25
- key_blocks: int32 [16, 8, 32, 8], P('dp', 'seq'), may hold values from 0 to 31, as said below
- key_count: int32 [16, 8, 32], P('dp', 'seq'), may hold values from 1 to 8, as said below
- cotangent: bfloat16 [16, 4096, 512], P('dp', 'seq'), may hold values from -6 to 6
Outputs:
- layer_out: bfloat16 [16, 4096, 512], P('dp', 'seq')
- grad_features: bfloat16 [16, 4096, 512], P('dp', 'seq')
- input_weight_grad: float32 [512, 1536], replicated
- output_weight_grad: float32 [512, 512], replicated
Inputs may be any that keep to these rules, and one draw needn't show every extreme that they name: `key_blocks`: slot 0 of query block i holds i; the other slots of one query block hold distinct blocks other than i. `key_count`: some query block of some head has 8 live slots in every draw.
All inputs are finite; a program needn't handle non-finite values.
Results may differ from a plain program's by a relative error of at most 0.029.
The roundings to bfloat16 on the way count: a program that leaves them out, or rounds other values in their place, can miss the bound.
Values may be sent and summed in bfloat16 or wider, within the bound.
A program may use at most 64 MiB of HBM per device.

v0:
```python
from functools import partial
import math

import jax
import jax.numpy as jnp
from jax import lax
from jax.sharding import PartitionSpec as P

H = 8
B = 128


NEGATIVE = -1e30


def block_probs(queries, key_tiles, live_count):
    scaling = queries.shape[0] ** (-0.5)
    scores = (
        jnp.einsum("eqr,eqjc->qrjc", queries, key_tiles, preferred_element_type=jnp.float32)
        * scaling
    )
    slot_ids = jnp.arange(key_tiles.shape[2])
    live_mask = (slot_ids[None, :] < live_count[:, None])[:, None, :, None]
    scores = jnp.where(live_mask, scores, NEGATIVE)
    highest = jnp.max(scores, axis=(2, 3), keepdims=True)
    raised = jnp.exp(scores - highest)
    return raised / jnp.sum(raised, axis=(2, 3), keepdims=True)


def head_forward(queries, keys_all, values_all, blocks, counts, per_step):
    num_steps = queries.shape[1] // per_step

    def advance(output, step_index):
        first_block = step_index * per_step
        query_block = lax.dynamic_slice_in_dim(queries, first_block, per_step, 1)
        chosen = lax.dynamic_slice_in_dim(blocks, first_block, per_step, 0)
        live_count = lax.dynamic_slice_in_dim(counts, first_block, per_step, 0)
        weights = block_probs(query_block, jnp.take(keys_all, chosen, axis=1), live_count).astype(
            jnp.bfloat16
        )
        attended = jnp.einsum(
            "qrjc,eqjc->eqr",
            weights,
            jnp.take(values_all, chosen, axis=1),
            preferred_element_type=jnp.float32,
        ).astype(jnp.bfloat16)
        return (lax.dynamic_update_slice_in_dim(output, attended, first_block, 1), None)

    return lax.scan(advance, jnp.zeros(queries.shape, jnp.bfloat16), jnp.arange(num_steps))[0]


def head_backward(queries, keys_all, values_all, attended, grad_attended, blocks, counts, per_step):
    num_steps = queries.shape[1] // per_step
    scaling = queries.shape[0] ** (-0.5)

    def advance(totals, step_index):
        grad_query, grad_keys, grad_values = totals
        first_block = step_index * per_step
        query_block = lax.dynamic_slice_in_dim(queries, first_block, per_step, 1)
        attended_block = lax.dynamic_slice_in_dim(attended, first_block, per_step, 1)
        grad_block = lax.dynamic_slice_in_dim(grad_attended, first_block, per_step, 1)
        chosen = lax.dynamic_slice_in_dim(blocks, first_block, per_step, 0)
        live_count = lax.dynamic_slice_in_dim(counts, first_block, per_step, 0)
        key_tiles = jnp.take(keys_all, chosen, axis=1)
        value_tiles = jnp.take(values_all, chosen, axis=1)
        weights_full = block_probs(query_block, key_tiles, live_count)
        weights = weights_full.astype(jnp.bfloat16)
        row_delta = jnp.sum(
            attended_block.astype(jnp.float32) * grad_block.astype(jnp.float32), axis=0
        )
        grad_probs = jnp.einsum(
            "eqr,eqjc->qrjc", grad_block, value_tiles, preferred_element_type=jnp.float32
        )
        grad_scores = (weights_full * (grad_probs - row_delta[:, :, None, None]) * scaling).astype(
            jnp.bfloat16
        )
        query_grad = jnp.einsum(
            "qrjc,eqjc->eqr", grad_scores, key_tiles, preferred_element_type=jnp.float32
        ).astype(jnp.bfloat16)
        grad_keys = grad_keys.at[:, chosen].add(
            jnp.einsum(
                "qrjc,eqr->eqjc", grad_scores, query_block, preferred_element_type=jnp.float32
            )
        )
        grad_values = grad_values.at[:, chosen].add(
            jnp.einsum("qrjc,eqr->eqjc", weights, grad_block, preferred_element_type=jnp.float32)
        )
        grad_query = lax.dynamic_update_slice_in_dim(grad_query, query_grad, first_block, 1)
        return ((grad_query, grad_keys, grad_values), None)

    start_totals = (
        jnp.zeros(queries.shape, jnp.bfloat16),
        jnp.zeros(keys_all.shape, jnp.float32),
        jnp.zeros(values_all.shape, jnp.float32),
    )
    grad_query, grad_keys, grad_values = lax.scan(advance, start_totals, jnp.arange(num_steps))[0]
    return (grad_query, grad_keys.astype(jnp.bfloat16), grad_values.astype(jnp.bfloat16))


def shards(features, input_weight, output_weight, key_blocks, key_count, cotangent):
    node_rows = features[0]
    grad_rows = cotangent[0]
    local_nodes, model_width = node_rows.shape
    seq_count = lax.axis_size("seq")
    span_nodes = local_nodes * seq_count
    block_count = span_nodes // B
    per_step = math.gcd(block_count, max(1, 512 // B))
    head_dim = model_width // H
    local_heads = H // seq_count
    proj_cols = (
        jnp.einsum("nd,dc->cn", node_rows, input_weight, preferred_element_type=jnp.float32)
        .astype(jnp.bfloat16)
        .reshape(3, model_width, local_nodes)
    )
    grad_cols = (
        jnp.einsum("fd,nd->fn", output_weight, grad_rows, preferred_element_type=jnp.float32)
        .astype(jnp.bfloat16)
        .reshape(1, model_width, local_nodes)
    )
    head_proj = lax.all_to_all(proj_cols, "seq", split_axis=1, concat_axis=2, tiled=True)
    head_tiles = head_proj.reshape(3, local_heads, head_dim, block_count, B)
    blocks_here = key_blocks[0]
    counts_here = key_count[0]
    attended = jax.vmap(partial(head_forward, per_step=per_step))(
        head_tiles[0], head_tiles[1], head_tiles[2], blocks_here, counts_here
    )
    back_rows = lax.all_to_all(
        attended.reshape(local_heads * head_dim, span_nodes),
        "seq",
        split_axis=1,
        concat_axis=0,
        tiled=True,
    )
    layer_out = (
        node_rows.astype(jnp.float32)
        + jnp.einsum("fn,fd->nd", back_rows, output_weight, preferred_element_type=jnp.float32)
    ).astype(jnp.bfloat16)
    head_grad = lax.all_to_all(grad_cols, "seq", split_axis=1, concat_axis=2, tiled=True)
    grad_tiles = head_grad.reshape(local_heads, head_dim, block_count, B)
    grad_query, grad_keys, grad_values = jax.vmap(partial(head_backward, per_step=per_step))(
        head_tiles[0], head_tiles[1], head_tiles[2], attended, grad_tiles, blocks_here, counts_here
    )
    stacked = jnp.stack([grad_query, grad_keys, grad_values]).reshape(
        3, local_heads * head_dim, span_nodes
    )
    node_grads = lax.all_to_all(stacked, "seq", split_axis=2, concat_axis=1, tiled=True).reshape(
        3 * model_width, local_nodes
    )
    grad_features = (
        grad_rows.astype(jnp.float32)
        + jnp.einsum("cn,dc->nd", node_grads, input_weight, preferred_element_type=jnp.float32)
    ).astype(jnp.bfloat16)
    input_terms = jnp.einsum("nd,cn->dc", node_rows, node_grads, preferred_element_type=jnp.float32)
    output_terms = jnp.einsum("fn,nd->fd", back_rows, grad_rows, preferred_element_type=jnp.float32)
    input_total, output_total = lax.psum((input_terms, output_terms), ("dp", "seq"))
    factor = 1.0 / math.sqrt(lax.axis_size("dp") * span_nodes)
    return (layer_out[None], grad_features[None], input_total * factor, output_total * factor)


def solution(mesh):
    in_specs = (
        P("dp", "seq", None),
        P(),
        P(),
        P("dp", "seq", None, None),
        P("dp", "seq", None),
        P("dp", "seq", None),
    )
    out_specs = (P("dp", "seq", None), P("dp", "seq", None), P(), P())
    return jax.shard_map(shards, mesh=mesh, in_specs=in_specs, out_specs=out_specs, check_vma=False)
```

profile of v0, /device:TPU:1, one launch (start us, length us, event | category | flops | bytes accessed | tf_op | source)
XLA Modules:
  0.0 673.6 jit_solution(819757375004870146)
XLA Ops:
  10.3 3.8 reduce.25
  15.3 6.0 all-to-all-start.2
  26.0 4.7 all-to-all-done.2
  30.8 5.1 all-to-all-start
  38.0 24.3 %all-to-all-done = bf16[3,512,512]{2,0,1:T(4,128)(2,1)} async-done(((bf16[3,512,512]{2,0,1:T(4,128)(2,1)}), bf16[3,512,512]{2,0,1:T(4,128)(2,1)}, u32[]{:S(2)}, u32[]{:S(2)}) %all-to-all-start) | async-done | bytes 1572896 | tf_op jit(solution)/shard_map/all_to_all | solution.py:120
  71.7 105.7 %while.34 = (s32[]{:T(128)}, bf16[1,64,32,128]{3,1,2,0:T(8,128)(2,1)}, s32[8]{0:T(128)S(1)}, s32[1,32,8]{2,1,0:T(8,128)S(1)}, bf16[1,64,32,128]{3,1,2,0:T(8,128)...) while((s32[]{:T(128)}, ...), condition=%wide.region_4.6_spmd, body=%wide.region_0.5_spmd.sunk | while | flops 141098496 | bytes 11745276 | solution.py:49
  182.6 256.9 %while.35 = (s32[]{:T(128)}, bf16[1,64,32,128]{3,2,1,0:T(8,128)(2,1)}, f32[1,64,32,128]{3,1,2,0:T(8,128)}, f32[1,64,32,128]{3,1,2,0:T(8,128)}, s32[8]{0:T(128)S(...) while((s32[]{:T(128)}, ...), condition=%wide.region_12.14_spmd, body=%wide.region_5.13_spmd.sunk | while | flops 347536576 | bytes 33053892 | solution.py:96
  202.1 4.8 scatter_fusion
  206.9 5.4 scatter_fusion.1
  234.3 4.8 scatter_fusion
  239.1 5.4 scatter_fusion.1
  266.4 4.8 scatter_fusion
  271.2 5.4 scatter_fusion.1
  298.5 4.8 scatter_fusion
  303.3 5.4 scatter_fusion.1
  330.6 4.8 scatter_fusion
  335.5 5.4 scatter_fusion.1
  362.8 4.8 scatter_fusion
  367.6 5.4 scatter_fusion.1
  394.9 4.8 scatter_fusion
  399.7 5.4 scatter_fusion.1
  426.9 4.8 scatter_fusion
  431.7 5.4 scatter_fusion.1
  445.4 4.9 all-to-all-start.1
  451.8 4.8 copy.115
  456.6 7.3 %reshape.660 = bf16[8,2,49152]{2,1,0:T(2,128)(2,1)} reshape(bf16[4096,3,64]{2,1,0:T(4,128)(2,1)} %bitcast.359) | data formatting | bytes 3145728
  463.8 4.8 all-to-all-start.3
  471.3 18.1 %all-to-all-done.3 = bf16[8,2,49152]{2,1,0:T(2,128)(2,1)S(1)} async-done(((bf16[8,2,49152]{2,1,0:T(2,128)(2,1)}), bf16[8,2,49152]{2,1,0:T(2,128)(2,1)S(1)}, u32[]{:S(2)}, u32[]{:S(2)}) %all-to-all-start.3) | async-done | bytes 1572896 | tf_op jit(solution)/shard_map/all_to_all | solution.py:146
  489.4 4.7 reshape.661
  494.1 5.4 copy.130
  507.8 150.4 %all-reduce.3.cloned.1.call-done = (f32[512,1536]{0,1:T(8,128)}, f32[512,512]{1,0:T(8,128)}) async-done(((f32[512,1536]{0,1:T(8,128)}, f32[512,512]{1,0:T(8,128)}), (f32[512,1536]{0,1:T(8,128)}, f32[512,512]{1,0:T(8,128)})) %all-reduce.3.cloned.1.call-update) | async-done | bytes 4194320 | tf_op jit(solution)/shard_map/psum | solution.py:155
  658.2 3.9 broadcast_multiply_fusion
  (527 shorter events, 317.6 us)
Async XLA Ops:
  7.2 14.1 %copy-start = (bf16[512,1536]{1,0:T(8,128)(2,1)S(1)}, bf16[512,1536]{1,0:T(8,128)(2,1)}, u32[]{:S(2)}) copy-start(bf16[512,1536]{1,0:T(8,128)(2,1)} %param.17) | copy-start | bytes 4718596
  15.3 15.5 %all-to-all-start.2 = ((bf16[8,2,16384]{2,1,0:T(2,128)(2,1)}), bf16[8,2,16384]{2,1,0:T(2,128)(2,1)S(1)}, u32[]{:S(2)}, u32[]{:S(2)}) async-start(bf16[8,2,16384]{2,1,0:T(2,128)(2,1)} %reshape.658), calls=%async_computation.2 | async-start | bytes 1048576 | tf_op jit(solution)/shard_map/all_to_all | solution.py:138
  26.0 9.8 %copy-start.12 = (s32[1,1,32,8]{2,3,1,0:T(8,128)S(1)}, s32[1,1,32,8]{2,3,1,0:T(8,128)}, u32[]{:S(2)}) copy-start(s32[1,1,32,8]{2,3,1,0:T(8,128)} %param.19) | copy-start | bytes 3076
  30.8 31.5 %all-to-all-start = ((bf16[3,512,512]{2,0,1:T(4,128)(2,1)}), bf16[3,512,512]{2,0,1:T(4,128)(2,1)}, u32[]{:S(2)}, u32[]{:S(2)}) async-start(bf16[3,512,512]{2,0,1:T(4,128)(2,1)} %copy.96), calls=%async_computation | async-start | bytes 4194304 | tf_op jit(solution)/shard_map/all_to_all | solution.py:120
  182.6 13.3 %copy-start.1 = (bf16[1,64,32,128]{3,1,2,0:T(8,128)(2,1)}, bf16[1,64,32,128]{3,1,2,0:T(8,128)(2,1)S(1)}, u32[]{:S(2)}) copy-start(bf16[1,64,32,128]{3,1,2,0:T(8,128)(2,1)S(1)} %get-tuple-element.613) | copy-start | bytes 1572868 | tf_op jit(solution)/shard_map/vmap()/while
  193.3 3.2 copy-start.5
  206.9 7.9 %copy-start.2 = (bf16[1,64,32,128]{3,1,2,0:T(8,128)(2,1)S(1)}, bf16[1,64,32,128]{3,1,2,0:T(8,128)(2,1)}, u32[]{:S(2)}) copy-start(bf16[1,64,32,128]{3,1,2,0:T(8,128)(2,1)} %copy-done.1) | copy-start | bytes 1572868 | tf_op jit(solution)/shard_map/vmap()/while
  214.8 13.3 %copy-start.1 = (bf16[1,64,32,128]{3,1,2,0:T(8,128)(2,1)}, bf16[1,64,32,128]{3,1,2,0:T(8,128)(2,1)S(1)}, u32[]{:S(2)}) copy-start(bf16[1,64,32,128]{3,1,2,0:T(8,128)(2,1)S(1)} %get-tuple-element.613) | copy-start | bytes 1572868 | tf_op jit(solution)/shard_map/vmap()/while
  225.5 3.2 copy-start.5
  239.0 7.9 %copy-start.2 = (bf16[1,64,32,128]{3,1,2,0:T(8,128)(2,1)S(1)}, bf16[1,64,32,128]{3,1,2,0:T(8,128)(2,1)}, u32[]{:S(2)}) copy-start(bf16[1,64,32,128]{3,1,2,0:T(8,128)(2,1)} %copy-done.1) | copy-start | bytes 1572868 | tf_op jit(solution)/shard_map/vmap()/while
  246.9 13.3 %copy-start.1 = (bf16[1,64,32,128]{3,1,2,0:T(8,128)(2,1)}, bf16[1,64,32,128]{3,1,2,0:T(8,128)(2,1)S(1)}, u32[]{:S(2)}) copy-start(bf16[1,64,32,128]{3,1,2,0:T(8,128)(2,1)S(1)} %get-tuple-element.613) | copy-start | bytes 1572868 | tf_op jit(solution)/shard_map/vmap()/while
  257.7 3.2 copy-start.5
  271.2 7.9 %copy-start.2 = (bf16[1,64,32,128]{3,1,2,0:T(8,128)(2,1)S(1)}, bf16[1,64,32,128]{3,1,2,0:T(8,128)(2,1)}, u32[]{:S(2)}) copy-start(bf16[1,64,32,128]{3,1,2,0:T(8,128)(2,1)} %copy-done.1) | copy-start | bytes 1572868 | tf_op jit(solution)/shard_map/vmap()/while
  279.0 13.3 %copy-start.1 = (bf16[1,64,32,128]{3,1,2,0:T(8,128)(2,1)}, bf16[1,64,32,128]{3,1,2,0:T(8,128)(2,1)S(1)}, u32[]{:S(2)}) copy-start(bf16[1,64,32,128]{3,1,2,0:T(8,128)(2,1)S(1)} %get-tuple-element.613) | copy-start | bytes 1572868 | tf_op jit(solution)/shard_map/vmap()/while
  289.8 3.2 copy-start.5
  303.3 7.9 %copy-start.2 = (bf16[1,64,32,128]{3,1,2,0:T(8,128)(2,1)S(1)}, bf16[1,64,32,128]{3,1,2,0:T(8,128)(2,1)}, u32[]{:S(2)}) copy-start(bf16[1,64,32,128]{3,1,2,0:T(8,128)(2,1)} %copy-done.1) | copy-start | bytes 1572868 | tf_op jit(solution)/shard_map/vmap()/while
  311.2 13.3 %copy-start.1 = (bf16[1,64,32,128]{3,1,2,0:T(8,128)(2,1)}, bf16[1,64,32,128]{3,1,2,0:T(8,128)(2,1)S(1)}, u32[]{:S(2)}) copy-start(bf16[1,64,32,128]{3,1,2,0:T(8,128)(2,1)S(1)} %get-tuple-element.613) | copy-start | bytes 1572868 | tf_op jit(solution)/shard_map/vmap()/while
  321.9 3.2 copy-start.5
  335.4 7.9 %copy-start.2 = (bf16[1,64,32,128]{3,1,2,0:T(8,128)(2,1)S(1)}, bf16[1,64,32,128]{3,1,2,0:T(8,128)(2,1)}, u32[]{:S(2)}) copy-start(bf16[1,64,32,128]{3,1,2,0:T(8,128)(2,1)} %copy-done.1) | copy-start | bytes 1572868 | tf_op jit(solution)/shard_map/vmap()/while
  343.3 13.3 %copy-start.1 = (bf16[1,64,32,128]{3,1,2,0:T(8,128)(2,1)}, bf16[1,64,32,128]{3,1,2,0:T(8,128)(2,1)S(1)}, u32[]{:S(2)}) copy-start(bf16[1,64,32,128]{3,1,2,0:T(8,128)(2,1)S(1)} %get-tuple-element.613) | copy-start | bytes 1572868 | tf_op jit(solution)/shard_map/vmap()/while
  354.0 3.2 copy-start.5
  367.6 7.9 %copy-start.2 = (bf16[1,64,32,128]{3,1,2,0:T(8,128)(2,1)S(1)}, bf16[1,64,32,128]{3,1,2,0:T(8,128)(2,1)}, u32[]{:S(2)}) copy-start(bf16[1,64,32,128]{3,1,2,0:T(8,128)(2,1)} %copy-done.1) | copy-start | bytes 1572868 | tf_op jit(solution)/shard_map/vmap()/while
  375.5 13.3 %copy-start.1 = (bf16[1,64,32,128]{3,1,2,0:T(8,128)(2,1)}, bf16[1,64,32,128]{3,1,2,0:T(8,128)(2,1)S(1)}, u32[]{:S(2)}) copy-start(bf16[1,64,32,128]{3,1,2,0:T(8,128)(2,1)S(1)} %get-tuple-element.613) | copy-start | bytes 1572868 | tf_op jit(solution)/shard_map/vmap()/while
  399.7 7.8 %copy-start.2 = (bf16[1,64,32,128]{3,1,2,0:T(8,128)(2,1)S(1)}, bf16[1,64,32,128]{3,1,2,0:T(8,128)(2,1)}, u32[]{:S(2)}) copy-start(bf16[1,64,32,128]{3,1,2,0:T(8,128)(2,1)} %copy-done.1) | copy-start | bytes 1572868 | tf_op jit(solution)/shard_map/vmap()/while
  407.5 13.3 %copy-start.1 = (bf16[1,64,32,128]{3,1,2,0:T(8,128)(2,1)}, bf16[1,64,32,128]{3,1,2,0:T(8,128)(2,1)S(1)}, u32[]{:S(2)}) copy-start(bf16[1,64,32,128]{3,1,2,0:T(8,128)(2,1)S(1)} %get-tuple-element.613) | copy-start | bytes 1572868 | tf_op jit(solution)/shard_map/vmap()/while
  418.2 3.2 copy-start.5
  431.7 7.8 %copy-start.2 = (bf16[1,64,32,128]{3,1,2,0:T(8,128)(2,1)S(1)}, bf16[1,64,32,128]{3,1,2,0:T(8,128)(2,1)}, u32[]{:S(2)}) copy-start(bf16[1,64,32,128]{3,1,2,0:T(8,128)(2,1)} %copy-done.1) | copy-start | bytes 1572868 | tf_op jit(solution)/shard_map/vmap()/while
  439.5 3.6 copy-start.6
  445.4 18.5 %all-to-all-start.1 = ((bf16[64,8,512]{2,0,1:T(8,128)(2,1)}), bf16[64,8,512]{2,0,1:T(8,128)(2,1)}, u32[]{:S(2)}, u32[]{:S(2)}) async-start(bf16[64,8,512]{2,0,1:T(8,128)(2,1)} %copy.105), calls=%async_computation.1 | async-start | bytes 1048576 | tf_op jit(solution)/shard_map/all_to_all | solution.py:127
  463.8 25.5 %all-to-all-start.3 = ((bf16[8,2,49152]{2,1,0:T(2,128)(2,1)}), bf16[8,2,49152]{2,1,0:T(2,128)(2,1)S(1)}, u32[]{:S(2)}, u32[]{:S(2)}) async-start(bf16[8,2,49152]{2,1,0:T(2,128)(2,1)} %reshape.660), calls=%async_computation.3 | async-start | bytes 3145728 | tf_op jit(solution)/shard_map/all_to_all | solution.py:146
  468.7 189.5 %all-reduce.3.cloned.1.call-start = ((), (), s32[]{:S(2)}) async-start(), calls=%async_computation.4 | async-start | bytes 8388608 | tf_op jit(solution)/shard_map/psum | solution.py:155
  662.1 3.6 copy-start.9
  (22 other events, 56.0 us)
Sparse Core Ops, SparseCore 0:
  503.4 154.7 all-reduce.2
where the time goes:
time: 679 us; the launch traced here: 674 us
  waiting for transfers between devices  198 us (29%)
  local copies, waits for them, and re-layouts  167 us (25%)
  other arithmetic  134 us (20%)
  matrix products  128 us (19%)
  starting transfers between devices  20.8 us (3%)
  between operations  14.2 us (2%)
  loops' own time  11.9 us (2%)
    psum x1, waiting for transfers between devices, shards(): lax.psum((input_terms, output_terms), ('dp', 'seq'))  150 us
    scatter-add x8, other arithmetic, advance(): grad_values.at[:, chosen]  43.5 us
    dot_general x16, matrix products, block_probs(): jnp.einsum('eqr,eqjc->qrjc', queries, key_tiles, preferred_element_type=j...  41.2 us
    scatter-add x16, other arithmetic, advance(): grad_keys.at[:, chosen]  38.3 us
    dot_general x8, matrix products, advance(): jnp.einsum('qrjc,eqjc->eqr', weights, jnp.take(values_all, chosen, axis=1...  28 us
    all_to_all x1, waiting for transfers between devices, shards(): lax.all_to_all(proj_cols, 'seq', split_axis=1, concat_axis=2, tiled=True)  24.3 us
    scatter x16, local copies, waits for them, and re-layouts, advance(): lax.dynamic_update_slice_in_dim(grad_query, query_grad, first_block, 1)  19.4 us
    while x8, local copies, waits for them, and re-layouts, advance(): lax.dynamic_slice_in_dim(grad_attended, first_block, per_step, 1)  18.3 us
  transfers between devices with their start and end apart: 5, of which 4 were waited for; matrix products, arithmetic and copies ran while one was open for 4% of the time, Pallas kernels for 0%

commit v1 on v0

v1 whole, which is shorter than its diff:
```python
from functools import partial

import jax
import jax.numpy as jnp
from jax import lax
from jax.experimental import pallas as pl
from jax.experimental.pallas import tpu as pltpu
from jax.sharding import PartitionSpec as P

H = 8
HD = 64
B = 128
KMAX = 8
NEGATIVE = -1e30
SCALE = HD**-0.5
MESH = pl.DeviceIdType.MESH
BF16 = jnp.bfloat16
F32 = jnp.float32
NN = (((1,), (0,)), ((), ()))
NT = (((1,), (1,)), ((), ()))
TN = (((0,), (0,)), ((), ()))
SIDE = 4


def dot(a, b, dims=NN):
    return lax.dot_general(a, b, dims, preferred_element_type=F32)


def seq_peers(seq):
    y, core = seq // 2, seq % 2
    peers = []
    for dy in (2, 1, 3):
        for flip in (0, 1):
            peers.append(((y + dy) % SIDE) * 2 + (core + flip) % 2)
    peers.append(y * 2 + (core + 1) % 2)
    return peers


def greet(devices):
    barrier = pltpu.get_barrier_semaphore()
    for device in devices:
        pl.semaphore_signal(barrier, inc=1, device_id=device, device_id_type=MESH)
    return lambda: pl.semaphore_wait(barrier, len(devices))


def project_kernel(
    x_ref, g_ref, wi_ref, wo_ref, kv_ref, qg_ref, kvt_ref, qgt_ref, kv_out, qg_out, send_sem, recv_sem
):
    dp, seq = lax.axis_index("dp"), lax.axis_index("seq")
    y, core = seq // 2, seq % 2
    nodes, width = x_ref.shape
    peers = seq_peers(seq)
    ready = greet([(dp, peer) for peer in peers])
    mine = pl.ds(pl.multiple_of(seq * nodes, nodes), nodes)

    def exchange(place, peer):
        copies = []
        for kind, (source, target) in enumerate(((kv_out, kv_ref), (qg_out, qg_ref))):
            copies.append(
                pltpu.make_async_remote_copy(
                    src_ref=source.at[place],
                    dst_ref=target.at[mine, :],
                    send_sem=send_sem.at[place, kind],
                    recv_sem=recv_sem.at[place, kind],
                    device_id=(dp, peer),
                    device_id_type=MESH,
                )
            )
        return copies

    copies = [exchange(place, peer) for place, peer in enumerate(peers)]
    for step, dy in enumerate((2, 1, 3, 0)):
        chip = (y + dy) % SIDE
        first = pl.multiple_of(chip * 2 * HD, 2 * HD)
        weights = jnp.concatenate(
            [wi_ref[:, pl.ds(pl.multiple_of(kind * width + first, 2 * HD), 2 * HD)] for kind in range(3)], 1
        )
        qkv = dot(x_ref[...], weights)
        q = (qkv[:, : 2 * HD] * SCALE).astype(BF16)
        k = qkv[:, 2 * HD : 4 * HD].astype(BF16)
        v = qkv[:, 4 * HD :].astype(BF16)
        g = dot(g_ref[...], wo_ref[pl.ds(first, 2 * HD), :], NT).astype(BF16)
        kv = [jnp.concatenate([k[:, :HD], v[:, :HD]], 1), jnp.concatenate([k[:, HD:], v[:, HD:]], 1)]
        qg = [jnp.concatenate([q[:, :HD], g[:, :HD]], 1), jnp.concatenate([q[:, HD:], g[:, HD:]], 1)]
        if dy:
            for c in (0, 1):
                place = 2 * step + (core + c) % 2
                kv_out[place], qg_out[place] = kv[c], qg[c]
            places = (2 * step, 2 * step + 1)
        else:
            same = core == 0
            kv_ref[mine, :], qg_ref[mine, :] = jnp.where(same, kv[0], kv[1]), jnp.where(same, qg[0], qg[1])
            kv_out[2 * step], qg_out[2 * step] = jnp.where(same, kv[1], kv[0]), jnp.where(same, qg[1], qg[0])
            places = (2 * step,)
        if step == 0:
            ready()
        for place in places:
            for copy in copies[place]:
                copy.start()

    def turn(source):
        here = pl.ds(pl.multiple_of(source * nodes, nodes), nodes)
        kvt_ref[:, here] = kv_ref[here, :].T
        qgt_ref[:, here] = qg_ref[here, :].T

    turn(seq)
    for place in (6, 2, 3, 4, 5, 0, 1):
        dy = (2, 2, 1, 1, 3, 3, 0)[place]
        flip = (0, 1, 0, 1, 0, 1, 1)[place]
        for copy in copies[place]:
            copy.wait_recv()
        turn(((y + SIDE - dy) % SIDE) * 2 + (core + flip) % 2)
    for pair in copies:
        for copy in pair:
            copy.wait_send()


def project(x, g, wi, wo):
    nodes, _ = x.shape
    span = nodes * H
    vm = pl.BlockSpec(memory_space=pltpu.VMEM)
    rows = jax.ShapeDtypeStruct((span, 2 * HD), BF16)
    cols = jax.ShapeDtypeStruct((2 * HD, span), BF16)
    return pl.pallas_call(
        project_kernel,
        out_shape=(rows, rows, cols, cols),
        in_specs=[vm] * 4,
        out_specs=(vm,) * 4,
        scratch_shapes=[
            pltpu.VMEM((H - 1, nodes, 2 * HD), BF16),
            pltpu.VMEM((H - 1, nodes, 2 * HD), BF16),
            pltpu.SemaphoreType.DMA((H - 1, 2)),
            pltpu.SemaphoreType.DMA((H - 1, 2)),
        ],
        compiler_params=pltpu.CompilerParams(collective_id=0, has_side_effects=True, vmem_limit_bytes=48 << 20),
        name="project",
    )(x, g, wi, wo)


def attention_kernel(group, blocks_ref, counts_ref, kv_ref, qg_ref, kvt_ref, qgt_ref, qa_ref, dkv_ref, total_ref):
    block_count = qg_ref.shape[0] // B
    total_ref[...] = jnp.zeros_like(total_ref)
    zero = jnp.zeros((HD, B), BF16)
    lane = lax.broadcasted_iota(jnp.int32, (B, B), 1)

    def query_block(i, live):
        here = pl.ds(pl.multiple_of(i * B, B), B)
        count = counts_ref[i]
        qg, qgt = qg_ref[here, :], qgt_ref[:, here]
        apart = jnp.concatenate(
            [jnp.concatenate([qgt[:HD], zero], 1), jnp.concatenate([zero, qgt[HD:]], 1)], 0
        )
        spots = [pl.ds(pl.multiple_of(blocks_ref[i, j] * B, B), B) for j in range(live)]
        kv = jnp.concatenate([kv_ref[spot, :] for spot in spots], 0)
        both = dot(kv, apart)
        scores = [both[:B, :B]]
        for j in range(1, live):
            scores.append(both[j * B : (j + 1) * B, :B] + jnp.where(j < count, 0.0, NEGATIVE))
        scores = jnp.concatenate(scores, 0)
        grad_probs = both[:, B:]
        raised = jnp.exp(scores - jnp.max(scores, 0, keepdims=True))
        inverse = 1.0 / jnp.sum(raised, 0, keepdims=True)
        row_delta = jnp.sum(raised * grad_probs, 0, keepdims=True) * inverse
        probs = raised * inverse
        weights = probs.astype(BF16)
        grad_scores = (probs * (grad_probs - row_delta)).astype(BF16)
        pair = jnp.concatenate([grad_scores, weights], 1)
        kvt = jnp.concatenate([kvt_ref[:, spot] for spot in spots], 1)
        out = dot(kvt, pair)
        out = jnp.concatenate([out[:HD, :B] * SCALE, out[HD:, B:]], 0)
        qa_ref[here, :] = out.T.astype(BF16)
        nothing = jnp.zeros_like(qg)
        split = jnp.concatenate([jnp.where(lane < HD, qg, nothing), jnp.where(lane < HD, nothing, qg)], 0)
        return spots, dot(pair, split)

    def step(index, carry):
        ids = [index * group + t for t in range(group)]
        most = counts_ref[ids[0]]
        for i in ids[1:]:
            most = jnp.maximum(most, counts_ref[i])
        for live in range(1, KMAX + 1):

            @pl.when(most == live)
            def _():
                for spots, terms in [query_block(i, live) for i in ids]:
                    for j, spot in enumerate(spots):
                        total_ref[spot, :] += terms[j * B : (j + 1) * B]

        return carry

    lax.fori_loop(0, block_count // group, step, 0)
    dkv_ref[...] = total_ref[...].astype(BF16)


def attention(blocks, counts, kv, qg, kvt, qgt):
    vm = pl.BlockSpec(memory_space=pltpu.VMEM)
    sm = pl.BlockSpec(memory_space=pltpu.SMEM)
    out = jax.ShapeDtypeStruct(kv.shape, BF16)
    return pl.pallas_call(
        partial(attention_kernel, 2),
        out_shape=(out, out),
        in_specs=[sm, sm, vm, vm, vm, vm],
        out_specs=(vm, vm),
        scratch_shapes=[pltpu.VMEM(kv.shape, F32)],
        compiler_params=pltpu.CompilerParams(vmem_limit_bytes=48 << 20),
        name="attention",
    )(blocks, counts, kv, qg, kvt, qgt)


ORDERS = (("x", "z", "y"), ("z", "x", "y"), ("y", "z", "x"), ("x", "y", "z"))
ROWS = (256, 64, 16, 16)


def finish_kernel(
    qa_ref, dkv_ref, x_ref, g_ref, wi_ref, wo_ref,
    layer_ref, gradf_ref, sums_ref,
    qa_in, dkv_in, grads, half_out, half_in, quarter_out, quarter_in, part_out, part_in, piece_out, piece_in,
    seq_send, seq_recv, core_send, core_recv, axis_send, axis_recv,
):
    dp, seq = lax.axis_index("dp"), lax.axis_index("seq")
    z, x, y, core = dp // SIDE, dp % SIDE, seq // 2, seq % 2
    place_of = {"x": x, "y": y, "z": z}
    nodes, width = x_ref.shape
    other = (dp, y * 2 + (core + 1) % 2)

    def along(axis, offset):
        if axis == "y":
            return (dp, ((y + offset) % SIDE) * 2 + core)
        if axis == "x":
            return (z * SIDE + (x + offset) % SIDE, seq)
        return (((z + offset) % SIDE) * SIDE + x, seq)

    peers = seq_peers(seq)
    greeted = [(dp, peer) for peer in peers]
    greeted += [along(axis, offset) for axis in ("x", "z") for offset in (1, 2, 3)]
    ready = greet(greeted)

    def remote(source, target, send, recv, device):
        return pltpu.make_async_remote_copy(
            src_ref=source, dst_ref=target, send_sem=send, recv_sem=recv, device_id=device, device_id_type=MESH
        )

    back = []
    for kind, (source, target) in enumerate(((qa_ref, qa_in), (dkv_ref, dkv_in))):
        for place, peer in enumerate(peers):
            rows = pl.ds(pl.multiple_of(peer * nodes, nodes), nodes)
            back.append(
                remote(
                    source.at[rows, :], target.at[seq], seq_send.at[kind, place], seq_recv.at[kind, place], (dp, peer)
                )
            )
    ready()
    for copy in back:
        copy.start()
    started = list(back)
    mine = pl.ds(pl.multiple_of(seq * nodes, nodes), nodes)
    qa_in[seq] = qa_ref[mine, :]
    dkv_in[seq] = dkv_ref[mine, :]
    turned = x_ref[...].T

    def heads(source, second):
        first = HD if second else 0
        return jnp.concatenate([source[head][:, first : first + HD] for head in range(H)], 1)

    def core_rows(c):
        return pl.ds(pl.multiple_of(c * ROWS[0], ROWS[0]), ROWS[0])

    def phase_core(m):
        half_out[m] = grads[m, core_rows(1 - core), :].astype(BF16)
        copy = remote(half_out.at[m], half_in.at[m], core_send.at[m, 0], core_recv.at[m, 0], other)
        copy.start()
        started.append(copy)
        return copy

    def start_axis(m, phase, sources, targets):
        copies = []
        for offset in (2, 1, 3):
            copy = remote(
                sources(offset),
                targets(offset),
                axis_send.at[m, phase, offset - 1],
                axis_recv.at[m, phase, offset - 1],
                along(ORDERS[m][min(phase, 5 - phase)], offset),
            )
            copy.start()
            copies.append(copy)
        started.extend(copies)
        return copies

    def phase_scatter(m, phase, waiting):
        place = place_of[ORDERS[m][phase]] if phase < 3 else None
        for copy in waiting:
            copy.wait_recv()
        if phase == 0:
            total = grads[m, core_rows(core), :] + half_in[m].astype(F32)
        elif phase == 1:
            total = (quarter_out_own[m] + quarter_in[m, 0].astype(F32)) + (
                quarter_in[m, 1].astype(F32) + quarter_in[m, 2].astype(F32)
            )
        elif phase == 2:
            total = (part_out_own[m] + part_in[m, 0].astype(F32)) + (
                part_in[m, 1].astype(F32) + part_in[m, 2].astype(F32)
            )
        else:
            return (piece_out_own[m] + piece_in[m, 0].astype(F32)) + (
                piece_in[m, 1].astype(F32) + piece_in[m, 2].astype(F32)
            )
        if phase == 0:
            grads[m, 0 : ROWS[0], :] = total
            rows = lambda p: pl.ds(pl.multiple_of(p * ROWS[1], ROWS[1]), ROWS[1])
            quarter_out[m] = total.astype(BF16)
            quarter_out_own[m] = grads[m, rows(place), :]
            return start_axis(
                m, 0, lambda o: quarter_out.at[m, rows((place + o) % SIDE), :], lambda o: quarter_in.at[m, o - 1]
            )
        if phase == 1:
            grads[m, 0 : ROWS[1], :] = total
            rows = lambda p: pl.ds(pl.multiple_of(p * ROWS[2], ROWS[2]), ROWS[2])
            part_out[m] = total.astype(BF16)
            part_out_own[m] = grads[m, rows(place), :]
            return start_axis(
                m, 1, lambda o: part_out.at[m, rows((place + o) % SIDE), :], lambda o: part_in.at[m, o - 1]
            )
        grads[m, 0 : ROWS[2], :] = total
        cols = lambda p: pl.ds(pl.multiple_of(p * B, B), B)
        piece_out[m] = total.astype(BF16)
        piece_out_own[m] = grads[m, 0 : ROWS[2], cols(place)]
        return start_axis(
            m, 2, lambda o: piece_out.at[m, :, cols((place + o) % SIDE)], lambda o: piece_in.at[m, o - 1]
        )

    quarter_out_own, part_out_own, piece_out_own = {}, {}, {}

    def spot(m, level):
        a, b, c = (place_of[axis] for axis in ORDERS[m])
        first = core * ROWS[0]
        if level >= 1:
            first = first + a * ROWS[1]
        if level >= 2:
            first = first + b * ROWS[2]
        rows = pl.ds(pl.multiple_of(first, ROWS[2]), ROWS[level])
        return (rows, pl.ds(pl.multiple_of(c * B, B), B)) if level == 3 else (rows, slice(None))

    def phase_gather(m, phase, waiting):
        for copy in waiting:
            copy.wait_recv()
        rows, cols = spot(m, 6 - phase)
        here = sums_ref.at[m, rows, cols]
        if phase < 6:
            return start_axis(m, phase, lambda o: here, lambda o: here)
        copy = remote(here, here, core_send.at[m, 1], core_recv.at[m, 1], other)
        copy.start()
        started.append(copy)
        return [copy]

    def advance(m, phase, waiting):
        if phase < 3:
            return phase_scatter(m, phase, waiting)
        if phase == 3:
            total = phase_scatter(m, 3, waiting)
            rows, cols = spot(m, 3)
            sums_ref[m, rows, cols] = total.astype(BF16)
            return phase_gather(m, 3, [])
        return phase_gather(m, phase, waiting)

    for copy in back[: H - 1]:
        copy.wait_recv()
    attended = heads(qa_in, True)
    grads[0] = dot(attended, g_ref[...], TN)
    waits = {0: [phase_core(0)]}
    grad_query = heads(qa_in, False)
    grads[1] = dot(turned, grad_query)
    waits[1] = [phase_core(1)]
    layer_ref[...] = (x_ref[...].astype(F32) + dot(attended, wo_ref[...])).astype(BF16)
    for m in (0, 1):
        waits[m] = advance(m, 0, waits[m])
    partial_grad = g_ref[...].astype(F32) + dot(grad_query, wi_ref[:, :width], NT)
    for copy in back[H - 1 :]:
        copy.wait_recv()
    grad_keys = heads(dkv_in, False)
    grads[2] = dot(turned, grad_keys)
    waits[2] = [phase_core(2)]
    grad_values = heads(dkv_in, True)
    grads[3] = dot(turned, grad_values)
    waits[3] = [phase_core(3)]
    partial_grad += dot(grad_keys, wi_ref[:, width : 2 * width], NT)
    for m in (2, 3):
        waits[m] = advance(m, 0, waits[m])
    partial_grad += dot(grad_values, wi_ref[:, 2 * width :], NT)
    gradf_ref[...] = partial_grad.astype(BF16)
    for phase in range(1, 7):
        for m in range(4):
            waits[m] = advance(m, phase, waits[m])
    for m in range(4):
        for copy in waits[m]:
            copy.wait_recv()
    for copy in started:
        copy.wait_send()


def finish(qa, dkv, x, g, wi, wo):
    nodes, width = x.shape
    vm = pl.BlockSpec(memory_space=pltpu.VMEM)
    rows = jax.ShapeDtypeStruct((nodes, width), BF16)
    return pl.pallas_call(
        finish_kernel,
        out_shape=(rows, rows, jax.ShapeDtypeStruct((4, width, width), BF16)),
        in_specs=[vm] * 6,
        out_specs=(vm,) * 3,
        scratch_shapes=[
            pltpu.VMEM((H, nodes, 2 * HD), BF16),
            pltpu.VMEM((H, nodes, 2 * HD), BF16),
            pltpu.VMEM((4, width, width), F32),
            pltpu.VMEM((4, ROWS[0], width), BF16),
            pltpu.VMEM((4, ROWS[0], width), BF16),
            pltpu.VMEM((4, ROWS[0], width), BF16),
            pltpu.VMEM((4, 3, ROWS[1], width), BF16),
            pltpu.VMEM((4, ROWS[1], width), BF16),
            pltpu.VMEM((4, 3, ROWS[2], width), BF16),
            pltpu.VMEM((4, ROWS[2], width), BF16),
            pltpu.VMEM((4, 3, ROWS[2], B), BF16),
            pltpu.SemaphoreType.DMA((2, H - 1)),
            pltpu.SemaphoreType.DMA((2, H - 1)),
            pltpu.SemaphoreType.DMA((4, 2)),
            pltpu.SemaphoreType.DMA((4, 2)),
            pltpu.SemaphoreType.DMA((4, 6, 3)),
            pltpu.SemaphoreType.DMA((4, 6, 3)),
        ],
        compiler_params=pltpu.CompilerParams(collective_id=1, has_side_effects=True, vmem_limit_bytes=48 << 20),
        name="finish",
    )(qa, dkv, x, g, wi, wo)


def shards(features, input_weight, output_weight, key_blocks, key_count, cotangent):
    x, g = features[0], cotangent[0]
    kv, qg, kvt, qgt = project(x, g, input_weight, output_weight)
    qa, dkv = attention(key_blocks[0, 0], key_count[0, 0], kv, qg, kvt, qgt)
    layer_out, grad_features, sums = finish(qa, dkv, x, g, input_weight, output_weight)
    factor = 1.0 / (lax.axis_size("dp") * lax.axis_size("seq") * x.shape[0]) ** 0.5
    input_total = jnp.concatenate([sums[1], sums[2], sums[3]], 1).astype(F32) * factor
    return (layer_out[None], grad_features[None], input_total, sums[0].astype(F32) * factor)


def solution(mesh):
    in_specs = (
        P("dp", "seq", None),
        P(),
        P(),
        P("dp", "seq", None, None),
        P("dp", "seq", None),
        P("dp", "seq", None),
    )
    out_specs = (P("dp", "seq", None), P("dp", "seq", None), P(), P())
    return jax.shard_map(shards, mesh=mesh, in_specs=in_specs, out_specs=out_specs, check_vma=False)
```

time: 679 us -> 127 us (0.19)
  waiting for transfers between devices: 198 us -> 0 us
  local copies, waits for them, and re-layouts: 167 us -> 7.91 us
  other arithmetic: 134 us -> 4.25 us
  matrix products: 128 us -> 0 us
  Pallas kernels: 0 us -> 113 us
  starting transfers between devices: 20.8 us -> 0 us
  between operations: 14.2 us -> 0.71 us
  loops' own time: 11.9 us -> 0 us
    psum x1 -> x0, waiting for transfers between devices: 150 us -> none  [shards(): lax.psum((input_terms, output_terms), ('dp', 'seq'))]
    dot_general x62 -> x0, matrix products: 128 us -> none  [the longest x16 41.2 us: block_probs(): jnp.einsum('eqr,eqjc->qrjc', queries, key_tiles, preferred_element_type=j...]
    pallas_call x0 -> x3, Pallas kernels: none -> 113 us  [the longest x1 61 us: finish(): pl.pallas_call(finish_kernel, out_shape=(rows, rows, jax.ShapeDtypeStruct...]
    scatter-add x24 -> x0, other arithmetic: 81.8 us -> none  [the longest x8 43.5 us: advance(): grad_values.at[:, chosen]]
    all_to_all x4 -> x0, waiting for transfers between devices: 47.2 us -> none  [the longest x1 24.3 us: shards(): lax.all_to_all(proj_cols, 'seq', split_axis=1, concat_axis=2, tiled=True)]
    gather x64 -> x0, local copies, waits for them, and re-layouts: 46.4 us -> none  [the longest x24 12 us: advance(): key_tiles = jnp.take(keys_all, chosen, axis=1)]
    while x108 -> x0, local copies, waits for them, and re-layouts: 30.9 us -> none  [the longest x8 18.3 us: advance(): lax.dynamic_slice_in_dim(grad_attended, first_block, per_step, 1)]
    another operation x24 -> x0, local copies, waits for them, and re-layouts: 21.3 us -> none
  transfers between devices with their start and end apart: 5 -> 0, of which waited for: 4 -> 0; matrix products, arithmetic and copies ran while one was open for 4% -> 0% of each run, Pallas kernels for 0% -> 0%
where the time goes in v1:
time: 127 us; the launch traced here: 126 us
  Pallas kernels  113 us (89%)
  local copies, waits for them, and re-layouts  7.91 us (6%)
  other arithmetic  4.25 us (3%)
    pallas_call x1, Pallas kernels, finish(): pl.pallas_call(finish_kernel, out_shape=(rows, rows, jax.ShapeDtypeStruct...  61 us
    pallas_call x1, Pallas kernels, project(): pl.pallas_call(project_kernel, out_shape=(rows, rows, cols, cols), in_spe...  31.4 us
    pallas_call x1, Pallas kernels, attention(): pl.pallas_call(partial(attention_kernel, 2), out_shape=(out, out), in_spe...  20.9 us
    unnamed x19, local copies, waits for them, and re-layouts  6.46 us

profile of v1, /device:TPU:1, one launch (start us, length us, event | category | flops | bytes accessed | tf_op | source)
XLA Modules:
  0.0 126.3 jit_solution(14239744488716932360)
XLA Ops:
  0.6 0.0 copy-start.7
  0.6 0.8 copy.10
  1.4 0.0 copy-start
  1.4 1.0 copy-done
  2.5 0.0 copy-start.2
  2.5 1.0 copy-done.2
  3.5 0.0 copy-start.4
  3.5 1.0 copy-done.4
  4.5 0.0 copy-start.1
  4.5 0.0 copy-start.3
  4.5 0.0 copy-start.5
  4.5 31.4 %project.1 = (bf16[4096,128]{1,0:T(8,128)(2,1)S(1)}, bf16[4096,128]{1,0:T(8,128)(2,1)S(1)}, bf16[128,4096]{1,0:T(8,128)(2,1)S(1)}, bf16[128,4096]{1,0:T(8,128)(2,1)S(1)}) custom-call(bf16[512,512]{1,0:T(8,128)(2,1)S(1)} %bitcast.14, bf16[512,512]{1,0:T(8,128)(2,1)S(1)} %bitcast.16, bf16[512,1536]{1,0:T(8,128)(2,1)} %wi_ref.3, bf16[512,512]{1,0:T(8,128)(2,1)S(1)} %copy-done.4), custom_call_target="tpu_custom_call" | custom-call | tf_op jit(solution)/shard_map/project/pallas_call | solution.py:124
  36.0 0.0 copy-start.6
  36.0 1.0 copy-done.6
  36.9 0.0 copy-done.7
  37.0 20.9 %attention.1 = (bf16[4096,128]{1,0:T(8,128)(2,1)S(1)}, bf16[4096,128]{1,0:T(8,128)(2,1)S(1)}) custom-call(s32[32,8]{1,0:T(8,128)S(1)} %bitcast.20, s32[32]{0:T(128)S(1)} %bitcast.21, bf16[4096,128]{1,0:T(8,128)(2,1)S(1)} %get-tuple-element.13.kv_ref, bf16[4096,128]{1,0:T(8,128)(2,1)S(1)} %get-tuple-element.14.qg_ref, ...), custom_call_target="tpu_custom_call" | custom-call | tf_op jit(solution)/shard_map/attention/pallas_call | solution.py:199
  57.9 0.0 copy-done.1
  57.9 0.0 copy-done.3
  57.9 0.0 copy-done.5
  57.9 61.0 %finish.1 = (bf16[512,512]{1,0:T(8,128)(2,1)S(1)}, bf16[512,512]{1,0:T(8,128)(2,1)S(1)}, bf16[4,512,512]{2,1,0:T(8,128)(2,1)}) custom-call(bf16[4096,128]{1,0:T(8,128)(2,1)S(1)} %get-tuple-element.17.qa_ref, bf16[4096,128]{1,0:T(8,128)(2,1)S(1)} %get-tuple-element.18.dkv_ref, bf16[512,512]{1,0:T(8,128)(2,1)S(1)} %bitcast.15, bf16[512,512]{1,0:T(8,128)(2,1)S(1)} %bitcast.17, ...), custom_call_target="tpu_custom_call" | custom-call | tf_op jit(solution)/shard_map/finish/pallas_call | solution.py:405
  119.0 2.2 %multiply_bitcast_fusion = f32[512,512]{1,0:T(8,128)} fusion(bf16[4,512,512]{2,1,0:T(8,128)(2,1)} %get-tuple-element.21), kind=kLoop, calls=%fused_computation.1 | loop fusion | flops 524288 | bytes 1572864 | tf_op jit(solution)/shard_map/mul | solution.py:441
  121.1 1.5 %slice_bitcast_fusion.2 = (bf16[512,512]{1,0:T(8,128)(2,1)S(1)}, bf16[512,512]{1,0:T(8,128)(2,1)S(1)}, bf16[512,512]{1,0:T(8,128)(2,1)S(1)}) fusion(bf16[4,512,512]{2,1,0:T(8,128)(2,1)} %get-tuple-element.21), kind=kLoop, calls=%fused_computation.4 | loop fusion | bytes 3145728 | tf_op jit(solution)/shard_map/squeeze | solution.py:440
  122.6 2.1 %convert_multiply_fusion = f32[512,1536]{1,0:T(8,128)} fusion(bf16[512,512]{1,0:T(8,128)(2,1)S(1)} %get-tuple-element.23, bf16[512,512]{1,0:T(8,128)(2,1)S(1)} %get-tuple-element.24, bf16[512,512]{1,0:T(8,128)(2,1)S(1)} %get-tuple-element.22), kind=kLoop, calls=%fused_computation | loop fusion | flops 5505024 | bytes 4718592 | tf_op jit(solution)/shard_map/mul | solution.py:440
  124.7 0.8 copy.13
  125.5 0.8 copy.14
Async XLA Ops:
  0.6 36.3 %copy-start.7 = (s32[1,1,32]{2,1,0:T(1,128)S(1)}, s32[1,1,32]{2,1,0:T(1,128)}, u32[]{:S(2)}) copy-start(s32[1,1,32]{2,1,0:T(1,128)} %param.10) | copy-start | bytes 388
  1.4 1.0 copy-start
  2.5 1.0 copy-start.2
  3.5 1.0 copy-start.4
  4.5 53.4 %copy-start.1 = (bf16[1,512,512]{2,1,0:T(8,128)(2,1)S(1)}, bf16[1,512,512]{2,1,0:T(8,128)(2,1)}, u32[]{:S(2)}) copy-start(bf16[1,512,512]{2,1,0:T(8,128)(2,1)} %param.6) | copy-start | bytes 1572868
  4.5 53.4 %copy-start.3 = (bf16[1,512,512]{2,1,0:T(8,128)(2,1)S(1)}, bf16[1,512,512]{2,1,0:T(8,128)(2,1)}, u32[]{:S(2)}) copy-start(bf16[1,512,512]{2,1,0:T(8,128)(2,1)} %param.11) | copy-start | bytes 1572868
  4.5 53.4 %copy-start.5 = (bf16[512,512]{1,0:T(8,128)(2,1)S(1)}, bf16[512,512]{1,0:T(8,128)(2,1)}, u32[]{:S(2)}) copy-start(bf16[512,512]{1,0:T(8,128)(2,1)} %wo_ref.3) | copy-start | bytes 1572868
  36.0 1.0 copy-start.6

commit v2 on v1

--- a/solution.py
+++ b/solution.py
@@ -43,8 +43,22 @@
     return lambda: pl.semaphore_wait(barrier, len(devices))
 
 
+def falling_order(counts):
+    size = counts.shape[1]
+    row = jnp.broadcast_to(counts.astype(F32), (size, size))
+    here = lax.broadcasted_iota(jnp.int32, (size, size), 0)
+    there = lax.broadcasted_iota(jnp.int32, (size, size), 1)
+    column = jnp.sum(jnp.where(here == there, row, 0.0), 1, keepdims=True)
+    ahead = (row > column) | ((row == column) & (there < here))
+    rank = jnp.sum(jnp.where(ahead, 1.0, 0.0), 1, keepdims=True)
+    found = jnp.where(rank == there.astype(F32), here.astype(F32), 0.0)
+    return jnp.sum(found, 0, keepdims=True).astype(jnp.int32)
+
+
 def project_kernel(
-    x_ref, g_ref, wi_ref, wo_ref, kv_ref, qg_ref, kvt_ref, qgt_ref, kv_out, qg_out, send_sem, recv_sem
+    x_ref, g_ref, wi_ref, wo_ref, count_ref,
+    kv_ref, qg_ref, kvt_ref, qgt_ref, order_ref,
+    kv_out, qg_out, send_sem, recv_sem,
 ):
     dp, seq = lax.axis_index("dp"), lax.axis_index("seq")
     y, core = seq // 2, seq % 2
@@ -104,6 +118,7 @@
         qgt_ref[:, here] = qg_ref[here, :].T
 
     turn(seq)
+    order_ref[...] = falling_order(count_ref[...])
     for place in (6, 2, 3, 4, 5, 0, 1):
         dy = (2, 2, 1, 1, 3, 3, 0)[place]
         flip = (0, 1, 0, 1, 0, 1, 1)[place]
@@ -115,7 +130,7 @@
             copy.wait_send()
 
 
-def project(x, g, wi, wo):
+def project(x, g, wi, wo, counts):
     nodes, _ = x.shape
     span = nodes * H
     vm = pl.BlockSpec(memory_space=pltpu.VMEM)
@@ -123,9 +138,9 @@
     cols = jax.ShapeDtypeStruct((2 * HD, span), BF16)
     return pl.pallas_call(
         project_kernel,
-        out_shape=(rows, rows, cols, cols),
-        in_specs=[vm] * 4,
-        out_specs=(vm,) * 4,
+        out_shape=(rows, rows, cols, cols, jax.ShapeDtypeStruct(counts.shape, jnp.int32)),
+        in_specs=[vm] * 5,
+        out_specs=(vm,) * 5,
         scratch_shapes=[
             pltpu.VMEM((H - 1, nodes, 2 * HD), BF16),
             pltpu.VMEM((H - 1, nodes, 2 * HD), BF16),
@@ -134,86 +149,90 @@
         ],
         compiler_params=pltpu.CompilerParams(collective_id=0, has_side_effects=True, vmem_limit_bytes=48 << 20),
         name="project",
-    )(x, g, wi, wo)
-
-
-def attention_kernel(group, blocks_ref, counts_ref, kv_ref, qg_ref, kvt_ref, qgt_ref, qa_ref, dkv_ref, total_ref):
+    )(x, g, wi, wo, counts)
+
+
+def attention_kernel(
+    group, order_ref, blocks_ref, counts_ref, kv_ref, qg_ref, kvt_ref, qgt_ref, qa_ref, dkv_ref, total_ref
+):
     block_count = qg_ref.shape[0] // B
     total_ref[...] = jnp.zeros_like(total_ref)
     zero = jnp.zeros((HD, B), BF16)
     lane = lax.broadcasted_iota(jnp.int32, (B, B), 1)
 
-    def query_block(i, live):
-        here = pl.ds(pl.multiple_of(i * B, B), B)
-        count = counts_ref[i]
-        qg, qgt = qg_ref[here, :], qgt_ref[:, here]
-        apart = jnp.concatenate(
-            [jnp.concatenate([qgt[:HD], zero], 1), jnp.concatenate([zero, qgt[HD:]], 1)], 0
-        )
-        spots = [pl.ds(pl.multiple_of(blocks_ref[i, j] * B, B), B) for j in range(live)]
-        kv = jnp.concatenate([kv_ref[spot, :] for spot in spots], 0)
-        both = dot(kv, apart)
-        scores = [both[:B, :B]]
-        for j in range(1, live):
-            scores.append(both[j * B : (j + 1) * B, :B] + jnp.where(j < count, 0.0, NEGATIVE))
-        scores = jnp.concatenate(scores, 0)
-        grad_probs = both[:, B:]
-        raised = jnp.exp(scores - jnp.max(scores, 0, keepdims=True))
-        inverse = 1.0 / jnp.sum(raised, 0, keepdims=True)
-        row_delta = jnp.sum(raised * grad_probs, 0, keepdims=True) * inverse
-        probs = raised * inverse
-        weights = probs.astype(BF16)
-        grad_scores = (probs * (grad_probs - row_delta)).astype(BF16)
-        pair = jnp.concatenate([grad_scores, weights], 1)
-        kvt = jnp.concatenate([kvt_ref[:, spot] for spot in spots], 1)
-        out = dot(kvt, pair)
-        out = jnp.concatenate([out[:HD, :B] * SCALE, out[HD:, B:]], 0)
-        qa_ref[here, :] = out.T.astype(BF16)
-        nothing = jnp.zeros_like(qg)
-        split = jnp.concatenate([jnp.where(lane < HD, qg, nothing), jnp.where(lane < HD, nothing, qg)], 0)
-        return spots, dot(pair, split)
+    def query_blocks(ids, live):
+        heres = [pl.ds(pl.multiple_of(i * B, B), B) for i in ids]
+        spots = [[pl.ds(pl.multiple_of(blocks_ref[i, j] * B, B), B) for j in range(live)] for i in ids]
+        products = []
+        for here, chosen in zip(heres, spots):
+            qgt = qgt_ref[:, here]
+            apart = jnp.concatenate(
+                [jnp.concatenate([qgt[:HD], zero], 1), jnp.concatenate([zero, qgt[HD:]], 1)], 0
+            )
+            products.append(dot(jnp.concatenate([kv_ref[spot, :] for spot in chosen], 0), apart))
+        pairs = []
+        for i, product in zip(ids, products):
+            count = counts_ref[i]
+            scores = [product[:B, :B]]
+            for j in range(1, live):
+                scores.append(product[j * B : (j + 1) * B, :B] + jnp.where(j < count, 0.0, NEGATIVE))
+            scores = jnp.concatenate(scores, 0)
+            grad_probs = product[:, B:]
+            raised = jnp.exp(scores - jnp.max(scores, 0, keepdims=True))
+            inverse = 1.0 / jnp.sum(raised, 0, keepdims=True)
+            row_delta = jnp.sum(raised * grad_probs, 0, keepdims=True) * inverse
+            probs = raised * inverse
+            grad_scores = (probs * (grad_probs - row_delta)).astype(BF16)
+            pairs.append(jnp.concatenate([grad_scores, probs.astype(BF16)], 1))
+        outs = []
+        for chosen, pair in zip(spots, pairs):
+            outs.append(dot(jnp.concatenate([kvt_ref[:, spot] for spot in chosen], 1), pair))
+        terms = []
+        for here, pair in zip(heres, pairs):
+            qg = qg_ref[here, :]
+            nothing = jnp.zeros_like(qg)
+            split = jnp.concatenate([jnp.where(lane < HD, qg, nothing), jnp.where(lane < HD, nothing, qg)], 0)
+            terms.append(dot(pair, split))
+        for here, out in zip(heres, outs):
+            both = jnp.concatenate([out[:HD, :B] * SCALE, out[HD:, B:]], 0)
+            qa_ref[here, :] = both.T.astype(BF16)
+        for chosen, term in zip(spots, terms):
+            for j, spot in enumerate(chosen):
+                total_ref[spot, :] += term[j * B : (j + 1) * B]
 
     def step(index, carry):
-        ids = [index * group + t for t in range(group)]
+        ids = [order_ref[0, index * group + t] for t in range(group)]
         most = counts_ref[ids[0]]
-        for i in ids[1:]:
-            most = jnp.maximum(most, counts_ref[i])
         for live in range(1, KMAX + 1):
-
-            @pl.when(most == live)
-            def _():
-                for spots, terms in [query_block(i, live) for i in ids]:
-                    for j, spot in enumerate(spots):
-                        total_ref[spot, :] += terms[j * B : (j + 1) * B]
-
+            pl.when(most == live)(partial(query_blocks, ids, live))
         return carry
 
     lax.fori_loop(0, block_count // group, step, 0)
     dkv_ref[...] = total_ref[...].astype(BF16)
 
 
-def attention(blocks, counts, kv, qg, kvt, qgt):
+def attention(order, blocks, counts, kv, qg, kvt, qgt):
     vm = pl.BlockSpec(memory_space=pltpu.VMEM)
     sm = pl.BlockSpec(memory_space=pltpu.SMEM)
     out = jax.ShapeDtypeStruct(kv.shape, BF16)
     return pl.pallas_call(
-        partial(attention_kernel, 2),
+        partial(attention_kernel, 4),
         out_shape=(out, out),
-        in_specs=[sm, sm, vm, vm, vm, vm],
+        in_specs=[sm, sm, sm, vm, vm, vm, vm],
         out_specs=(vm, vm),
         scratch_shapes=[pltpu.VMEM(kv.shape, F32)],
-        compiler_params=pltpu.CompilerParams(vmem_limit_bytes=48 << 20),
+        compiler_params=pltpu.CompilerParams(vmem_limit_bytes=56 << 20),
         name="attention",
-    )(blocks, counts, kv, qg, kvt, qgt)
+    )(order, blocks, counts, kv, qg, kvt, qgt)
 
 
 ORDERS = (("x", "z", "y"), ("z", "x", "y"), ("y", "z", "x"), ("x", "y", "z"))
-ROWS = (256, 64, 16, 16)
+ROWS = (256, 64, 16)
 
 
 def finish_kernel(
     qa_ref, dkv_ref, x_ref, g_ref, wi_ref, wo_ref,
-    layer_ref, gradf_ref, sums_ref,
+    layer_ref, gradf_ref, osum_ref, isum_ref,
     qa_in, dkv_in, grads, half_out, half_in, quarter_out, quarter_in, part_out, part_in, piece_out, piece_in,
     seq_send, seq_recv, core_send, core_recv, axis_send, axis_recv,
 ):
@@ -272,7 +291,7 @@
         started.append(copy)
         return copy
 
-    def start_axis(m, phase, sources, targets):
+    def start_axis(m, phase, level, sources, targets):
         copies = []
         for offset in (2, 1, 3):
             copy = remote(
@@ -280,7 +299,7 @@
                 targets(offset),
                 axis_send.at[m, phase, offset - 1],
                 axis_recv.at[m, phase, offset - 1],
-                along(ORDERS[m][min(phase, 5 - phase)], offset),
+                along(ORDERS[m][level], offset),
             )
             copy.start()
             copies.append(copy)
@@ -302,8 +321,8 @@
                 part_in[m, 1].astype(F32) + part_in[m, 2].astype(F32)
             )
         else:
-            return (piece_out_own[m] + piece_in[m, 0].astype(F32)) + (
-                piece_in[m, 1].astype(F32) + piece_in[m, 2].astype(F32)
+            return (piece_in[m, 0].astype(F32) + piece_in[m, 1].astype(F32)) + (
+                piece_in[m, 2].astype(F32) + piece_in[m, 3].astype(F32)
             )
         if phase == 0:
             grads[m, 0 : ROWS[0], :] = total
@@ -311,7 +330,7 @@
             quarter_out[m] = total.astype(BF16)
             quarter_out_own[m] = grads[m, rows(place), :]
             return start_axis(
-                m, 0, lambda o: quarter_out.at[m, rows((place + o) % SIDE), :], lambda o: quarter_in.at[m, o - 1]
+                m, 0, 0, lambda o: quarter_out.at[m, rows((place + o) % SIDE), :], lambda o: quarter_in.at[m, o - 1]
             )
         if phase == 1:
             grads[m, 0 : ROWS[1], :] = total
@@ -319,35 +338,30 @@
             part_out[m] = total.astype(BF16)
             part_out_own[m] = grads[m, rows(place), :]
             return start_axis(
-                m, 1, lambda o: part_out.at[m, rows((place + o) % SIDE), :], lambda o: part_in.at[m, o - 1]
-            )
-        grads[m, 0 : ROWS[2], :] = total
-        cols = lambda p: pl.ds(pl.multiple_of(p * B, B), B)
+                m, 1, 1, lambda o: part_out.at[m, rows((place + o) % SIDE), :], lambda o: part_in.at[m, o - 1]
+            )
         piece_out[m] = total.astype(BF16)
-        piece_out_own[m] = grads[m, 0 : ROWS[2], cols(place)]
-        return start_axis(
-            m, 2, lambda o: piece_out.at[m, :, cols((place + o) % SIDE)], lambda o: piece_in.at[m, o - 1]
-        )
-
-    quarter_out_own, part_out_own, piece_out_own = {}, {}, {}
-
-    def spot(m, level):
-        a, b, c = (place_of[axis] for axis in ORDERS[m])
+        piece_in[m, place] = total.astype(BF16)
+        return start_axis(m, 2, 2, lambda o: piece_out.at[m], lambda o: piece_in.at[m, place])
+
+    quarter_out_own, part_out_own = {}, {}
+
+    def region(m, level):
+        a, b = (place_of[axis] for axis in ORDERS[m][:2])
         first = core * ROWS[0]
         if level >= 1:
             first = first + a * ROWS[1]
         if level >= 2:
             first = first + b * ROWS[2]
         rows = pl.ds(pl.multiple_of(first, ROWS[2]), ROWS[level])
-        return (rows, pl.ds(pl.multiple_of(c * B, B), B)) if level == 3 else (rows, slice(None))
+        return osum_ref.at[rows, :] if m == 0 else isum_ref.at[rows, pl.ds((m - 1) * width, width)]
 
     def phase_gather(m, phase, waiting):
         for copy in waiting:
             copy.wait_recv()
-        rows, cols = spot(m, 6 - phase)
-        here = sums_ref.at[m, rows, cols]
-        if phase < 6:
-            return start_axis(m, phase, lambda o: here, lambda o: here)
+        here = region(m, 5 - phase)
+        if phase < 5:
+            return start_axis(m, phase, 4 - phase, lambda o: here, lambda o: here)
         copy = remote(here, here, core_send.at[m, 1], core_recv.at[m, 1], other)
         copy.start()
         started.append(copy)
@@ -358,9 +372,8 @@
             return phase_scatter(m, phase, waiting)
         if phase == 3:
             total = phase_scatter(m, 3, waiting)
-            rows, cols = spot(m, 3)
-            sums_ref[m, rows, cols] = total.astype(BF16)
-            return phase_gather(m, 3, [])
+            region(m, 2)[...] = total.astype(BF16)
+            waiting = []
         return phase_gather(m, phase, waiting)
 
     for copy in back[: H - 1]:
@@ -374,6 +387,9 @@
     layer_ref[...] = (x_ref[...].astype(F32) + dot(attended, wo_ref[...])).astype(BF16)
     for m in (0, 1):
         waits[m] = advance(m, 0, waits[m])
+    for phase in (1, 2):
+        for m in (0, 1):
+            waits[m] = advance(m, phase, waits[m])
     partial_grad = g_ref[...].astype(F32) + dot(grad_query, wi_ref[:, :width], NT)
     for copy in back[H - 1 :]:
         copy.wait_recv()
@@ -383,14 +399,19 @@
     grad_values = heads(dkv_in, True)
     grads[3] = dot(turned, grad_values)
     waits[3] = [phase_core(3)]
-    partial_grad += dot(grad_keys, wi_ref[:, width : 2 * width], NT)
+    for m in (0, 1):
+        waits[m] = advance(m, 3, waits[m])
     for m in (2, 3):
         waits[m] = advance(m, 0, waits[m])
+    partial_grad += dot(grad_keys, wi_ref[:, width : 2 * width], NT)
     partial_grad += dot(grad_values, wi_ref[:, 2 * width :], NT)
     gradf_ref[...] = partial_grad.astype(BF16)
-    for phase in range(1, 7):
-        for m in range(4):
+    for phase in range(1, 6):
+        for m in (2, 3):
             waits[m] = advance(m, phase, waits[m])
+        if phase in (1, 2):
+            for m in (0, 1):
+                waits[m] = advance(m, phase + 3, waits[m])
     for m in range(4):
         for copy in waits[m]:
             copy.wait_recv()
@@ -404,9 +425,14 @@
     rows = jax.ShapeDtypeStruct((nodes, width), BF16)
     return pl.pallas_call(
         finish_kernel,
-        out_shape=(rows, rows, jax.ShapeDtypeStruct((4, width, width), BF16)),
+        out_shape=(
+            rows,
+            rows,
+            jax.ShapeDtypeStruct((width, width), BF16),
+            jax.ShapeDtypeStruct((width, 3 * width), BF16),
+        ),
         in_specs=[vm] * 6,
-        out_specs=(vm,) * 3,
+        out_specs=(vm,) * 4,
         scratch_shapes=[
             pltpu.VMEM((H, nodes, 2 * HD), BF16),
             pltpu.VMEM((H, nodes, 2 * HD), BF16),
@@ -418,13 +444,13 @@
             pltpu.VMEM((4, ROWS[1], width), BF16),
             pltpu.VMEM((4, 3, ROWS[2], width), BF16),
             pltpu.VMEM((4, ROWS[2], width), BF16),
-            pltpu.VMEM((4, 3, ROWS[2], B), BF16),
+            pltpu.VMEM((4, SIDE, ROWS[2], width), BF16),
             pltpu.SemaphoreType.DMA((2, H - 1)),
             pltpu.SemaphoreType.DMA((2, H - 1)),
             pltpu.SemaphoreType.DMA((4, 2)),
             pltpu.SemaphoreType.DMA((4, 2)),
-            pltpu.SemaphoreType.DMA((4, 6, 3)),
-            pltpu.SemaphoreType.DMA((4, 6, 3)),
+            pltpu.SemaphoreType.DMA((4, 5, 3)),
+            pltpu.SemaphoreType.DMA((4, 5, 3)),
         ],
         compiler_params=pltpu.CompilerParams(collective_id=1, has_side_effects=True, vmem_limit_bytes=48 << 20),
         name="finish",
@@ -433,12 +459,11 @@
 
 def shards(features, input_weight, output_weight, key_blocks, key_count, cotangent):
     x, g = features[0], cotangent[0]
-    kv, qg, kvt, qgt = project(x, g, input_weight, output_weight)
-    qa, dkv = attention(key_blocks[0, 0], key_count[0, 0], kv, qg, kvt, qgt)
-    layer_out, grad_features, sums = finish(qa, dkv, x, g, input_weight, output_weight)
+    kv, qg, kvt, qgt, order = project(x, g, input_weight, output_weight, key_count[0])
+    qa, dkv = attention(order, key_blocks[0, 0], key_count[0, 0], kv, qg, kvt, qgt)
+    layer_out, grad_features, osum, isum = finish(qa, dkv, x, g, input_weight, output_weight)
     factor = 1.0 / (lax.axis_size("dp") * lax.axis_size("seq") * x.shape[0]) ** 0.5
-    input_total = jnp.concatenate([sums[1], sums[2], sums[3]], 1).astype(F32) * factor
-    return (layer_out[None], grad_features[None], input_total, sums[0].astype(F32) * factor)
+    return (layer_out[None], grad_features[None], isum.astype(F32) * factor, osum.astype(F32) * factor)
 
 
 def solution(mesh):

time: 127 us -> 132 us (1.039)
  local copies, waits for them, and re-layouts: 7.91 us -> 12.9 us
    pallas_call x1, Pallas kernels: 61 us -> 69.4 us  [finish(): pl.pallas_call(finish_kernel, out_shape=(rows, rows, jax.ShapeDtypeStruct...]
    pallas_call x2, Pallas kernels: 52.4 us -> 44.4 us  [the longest x1 31.4 us: project(): pl.pallas_call(project_kernel, out_shape=(rows, rows, cols, cols, jax.Sha...]
    unnamed x19 -> x33, local copies, waits for them, and re-layouts: 6.46 us -> 12.9 us
    squeeze x1 -> x0, local copies, waits for them, and re-layouts: 1.46 us -> none  [shards(): sums[1]]
where the time goes in v2:
time: 132 us
  Pallas kernels  114 us (86%)
  local copies, waits for them, and re-layouts  12.9 us (10%)
  other arithmetic  4.61 us (3%)
    pallas_call x1, Pallas kernels, finish(): pl.pallas_call(finish_kernel, out_shape=(rows, rows, jax.ShapeDtypeStruct...  69.4 us
    pallas_call x1, Pallas kernels, project(): pl.pallas_call(project_kernel, out_shape=(rows, rows, cols, cols, jax.Sha...  31.4 us
    pallas_call x1, Pallas kernels, attention(): pl.pallas_call(partial(attention_kernel, 4), out_shape=(out, out), in_spe...  13 us
    unnamed x33, local copies, waits for them, and re-layouts  12.9 us
    mul x1, other arithmetic, shards(): isum.astype(F32) * factor  3.5 us

profile of v2, /device:TPU:1, one launch (start us, length us, event | category | flops | bytes accessed | tf_op | source)
XLA Modules:
  0.0 132.1 jit_solution(15501336000621241735)
XLA Ops:
  0.6 0.0 copy-start.14
  0.6 0.0 copy-start
  0.7 1.0 copy-done
  1.7 0.0 copy-start.2
  1.7 1.0 copy-done.2
  2.7 0.0 copy-start.4
  2.7 1.0 copy-done.4
  3.8 0.0 copy-start.12
  3.8 0.7 copy-done.12
  4.4 0.0 copy-start.1
  4.4 0.0 copy-start.3
  4.4 31.4 %project.1 = (bf16[4096,128]{1,0:T(8,128)(2,1)S(1)}, bf16[4096,128]{1,0:T(8,128)(2,1)S(1)}, bf16[128,4096]{1,0:T(8,128)(2,1)S(1)}, bf16[128,4096]{1,0:T(8,128)(2,1)S(1)}, s32[1,32]{1,0:T(1,128)S(1)}) custom-call(bf16[512,512]{1,0:T(8,128)(2,1)S(1)} %bitcast.7, bf16[512,512]{1,0:T(8,128)(2,1)S(1)} %bitcast.9, bf16[512,1536]{1,0:T(8,128)(2,1)} %wi_ref.3, ...), custom_call_target="tpu_custom_call" | custom-call | tf_op jit(solution)/shard_map/project/pallas_call | solution.py:139
  35.9 0.0 copy-start.8
  35.9 1.0 copy-done.8
  36.8 1.0 copy-done.9
  37.8 1.0 copy-done.10
  38.8 1.0 copy-done.11
  39.8 0.5 copy-done.13
  40.3 0.0 copy-done.14
  40.3 0.7 copy.10
  41.0 13.0 %attention.1 = (bf16[4096,128]{1,0:T(8,128)(2,1)}, bf16[4096,128]{1,0:T(8,128)(2,1)}) custom-call(s32[1,32]{1,0:T(1,128)} %copy-done.13, s32[32,8]{1,0:T(8,128)} %bitcast.15, s32[32]{0:T(128)} %bitcast.13, bf16[4096,128]{1,0:T(8,128)(2,1)} %copy-done.8, bf16[4096,128]{1,0:T(8,128)(2,1)} %copy-done.9, bf16[128,4096]{1,0:T(8,128)(2,1)} %copy-done.10, ...), custom_call_target="tpu_custom_call" | custom-call | tf_op jit(solution)/shard_map/attention/pallas_call | solution.py:218
  54.0 0.0 copy-done.1
  54.0 0.0 copy-done.3
  54.0 0.0 copy-done.5
  54.0 0.0 copy-start.6
  54.0 1.2 copy-done.6
  55.2 1.2 copy-done.7
  56.4 69.4 %finish.1 = (bf16[512,512]{1,0:T(8,128)(2,1)S(1)}, bf16[512,512]{1,0:T(8,128)(2,1)S(1)}, bf16[512,512]{1,0:T(8,128)(2,1)S(1)}, bf16[512,1536]{1,0:T(8,128)(2,1)}) custom-call(bf16[4096,128]{1,0:T(8,128)(2,1)S(1)} %copy-done.6, bf16[4096,128]{1,0:T(8,128)(2,1)S(1)} %copy-done.7, bf16[512,512]{1,0:T(8,128)(2,1)S(1)} %bitcast.8, bf16[512,512]{1,0:T(8,128)(2,1)S(1)} %bitcast.10, ...), custom_call_target="tpu_custom_call" | custom-call | tf_op jit(solution)/shard_map/finish/pallas_call | solution.py:426
  125.9 3.5 %convert_multiply_fusion = f32[512,1536]{1,0:T(8,128)} fusion(bf16[512,1536]{1,0:T(8,128)(2,1)} %get-tuple-element.24), kind=kLoop, calls=%fused_computation | loop fusion | flops 1572864 | bytes 4718592 | tf_op jit(solution)/shard_map/mul | solution.py:466
  129.4 1.1 convert_multiply_fusion.1
  130.5 0.8 copy.13
  131.3 0.8 copy.14
  (6 shorter events, 0.0 us)
Async XLA Ops:
  0.6 39.7 %copy-start.14 = (s32[1,1,32,8]{2,3,1,0:T(8,128)S(1)}, s32[1,1,32,8]{2,3,1,0:T(8,128)}, u32[]{:S(2)}) copy-start(s32[1,1,32,8]{2,3,1,0:T(8,128)} %param.9) | copy-start | bytes 3076
  0.6 1.0 copy-start
  1.7 1.0 copy-start.2
  2.7 1.0 copy-start.4
  3.8 0.7 copy-start.12
  4.4 49.5 %copy-start.1 = (bf16[1,512,512]{2,1,0:T(8,128)(2,1)S(1)}, bf16[1,512,512]{2,1,0:T(8,128)(2,1)}, u32[]{:S(2)}) copy-start(bf16[1,512,512]{2,1,0:T(8,128)(2,1)} %param.6) | copy-start | bytes 1572868
  4.4 49.5 %copy-start.3 = (bf16[1,512,512]{2,1,0:T(8,128)(2,1)S(1)}, bf16[1,512,512]{2,1,0:T(8,128)(2,1)}, u32[]{:S(2)}) copy-start(bf16[1,512,512]{2,1,0:T(8,128)(2,1)} %param.11) | copy-start | bytes 1572868
  4.4 49.5 %copy-start.5 = (bf16[512,512]{1,0:T(8,128)(2,1)S(1)}, bf16[512,512]{1,0:T(8,128)(2,1)}, u32[]{:S(2)}) copy-start(bf16[512,512]{1,0:T(8,128)(2,1)} %wo_ref.3) | copy-start | bytes 1572868
  35.9 1.0 copy-start.8
  36.8 1.0 copy-start.9
  37.8 1.0 copy-start.10
  38.8 1.0 copy-start.11
  39.8 0.5 copy-start.13
  54.0 1.2 copy-start.6
  55.2 1.2 copy-start.7

commit v3 on v0

v3 whole, which is shorter than its diff:
```python
from functools import partial

import jax
import jax.numpy as jnp
from jax import lax
from jax.experimental import pallas as pl
from jax.experimental.pallas import tpu as pltpu
from jax.sharding import PartitionSpec as P

H = 8
HD = 64
B = 128
KMAX = 8
NEGATIVE = -1e30
SCALE = HD**-0.5
MESH = pl.DeviceIdType.MESH
BF16 = jnp.bfloat16
F32 = jnp.float32
NN = (((1,), (0,)), ((), ()))
NT = (((1,), (1,)), ((), ()))
TN = (((0,), (0,)), ((), ()))
SIDE = 4
VMEM_BYTES = 60 << 20


def dot(a, b, dims=NN):
    return lax.dot_general(a, b, dims, preferred_element_type=F32)


def part(index, size):
    return pl.ds(pl.multiple_of(index * size, size), size)


def seq_peers(seq):
    y, core = seq // 2, seq % 2
    peers = []
    for dy in (2, 1, 3):
        for flip in (0, 1):
            peers.append(((y + dy) % SIDE) * 2 + (core + flip) % 2)
    peers.append(y * 2 + (core + 1) % 2)
    return peers


def greet(devices):
    barrier = pltpu.get_barrier_semaphore()
    for device in devices:
        pl.semaphore_signal(barrier, inc=1, device_id=device, device_id_type=MESH)
    pl.semaphore_wait(barrier, len(devices))


def remote(source, target, sems, index, device):
    return pltpu.make_async_remote_copy(
        src_ref=source,
        dst_ref=target,
        send_sem=sems[0].at[index],
        recv_sem=sems[1].at[index],
        device_id=device,
        device_id_type=MESH,
    )


def falling_order(counts):
    size = counts.shape[1]
    row = jnp.broadcast_to(counts.astype(F32), (size, size))
    here = lax.broadcasted_iota(jnp.int32, (size, size), 0)
    there = lax.broadcasted_iota(jnp.int32, (size, size), 1)
    column = jnp.sum(jnp.where(here == there, row, 0.0), 1, keepdims=True)
    ahead = (row > column) | ((row == column) & (there < here))
    rank = jnp.sum(jnp.where(ahead, 1.0, 0.0), 1, keepdims=True)
    found = jnp.where(rank == there.astype(F32), here.astype(F32), 0.0)
    return jnp.sum(found, 0, keepdims=True).astype(jnp.int32)


def project_kernel(
    x_hbm, g_hbm, wi_hbm, wo_hbm, count_ref,
    kv_ref, kvt_ref, qgt_ref, order_ref, all_hbm,
    x_ref, g_ref, wi_ref, wo_ref, gt_ref, send_sem, recv_sem, load_sem, store_sem,
):
    dp, seq = lax.axis_index("dp"), lax.axis_index("seq")
    y, core = seq // 2, seq % 2
    nodes, width = g_ref.shape
    half = nodes // 2
    sems = (send_sem, recv_sem)
    other = (dp, y * 2 + (core + 1) % 2)

    def at(dy, flip=0):
        return ((y + dy) % SIDE) * 2 + (core + flip) % 2

    loads = [
        pltpu.make_async_copy(source, target, load_sem.at[k])
        for k, (source, target) in enumerate(
            ((x_hbm, x_ref.at[seq]), (g_hbm, g_ref), (wi_hbm, wi_ref), (wo_hbm, wo_ref))
        )
    ]
    for load in loads:
        load.start()
    peers = seq_peers(seq)
    greet([(dp, peer) for peer in peers])
    up, down = (dp, at(1)), (dp, at(3))

    def rows(h):
        return pl.ds(h * half, half)

    def pass_on(source, h, index, device):
        piece = x_ref.at[source, rows(h)]
        return remote(piece, piece, sems, index, device)

    def own(h, index, device):
        return remote(x_hbm.at[rows(h)], x_ref.at[seq, rows(h)], sems, index, device)

    sent = [own(0, 0, up), own(1, 3, down), own(1, 1, up), own(0, 4, down), own(0, 6, other), own(1, 7, other)]
    for copy in sent:
        copy.start()

    loads[1].wait()
    loads[3].wait()
    gt_ref[...] = dot(wo_ref[...], g_ref[...], NT).astype(BF16)
    head_rows = pl.ds(HD, HD)
    given = []
    for place, peer in enumerate(peers):
        given.append(
            remote(gt_ref.at[part(peer, HD), :], qgt_ref.at[head_rows, part(seq, nodes)], sems, 14 + place, (dp, peer))
        )
        given[-1].start()
    qgt_ref[head_rows, part(seq, nodes)] = gt_ref[part(seq, HD), :]
    loads[2].wait()
    loads[0].wait()
    chosen = []
    for kind in (1, 2, 0):
        block = wi_ref[:, pl.ds(pl.multiple_of(kind * width + y * 2 * HD, 2 * HD), 2 * HD)]
        chosen.append(jnp.where(core == 0, block[:, :HD], block[:, HD:]))
    chosen[2] = chosen[2] * jnp.asarray(SCALE, BF16)
    weights = jnp.concatenate(chosen + [jnp.zeros_like(chosen[0])], 1)
    stores = []

    def project_half(source, h):
        place = 2 * source + h
        here = part(place, half)
        product = dot(x_ref[source, rows(h), :], weights)
        kv = product[:, : 2 * HD].astype(BF16)
        kv_ref[here, :] = kv
        kvt_ref[:, here] = kv.T
        qgt_ref[:HD, here] = product[:, 2 * HD :].T[:HD].astype(BF16)
        store = pltpu.make_async_copy(x_ref.at[source, rows(h)], all_hbm.at[here, :], store_sem.at[len(stores)])
        store.start()
        stores.append(store)

    project_half(seq, 0)
    project_half(seq, 1)
    order_ref[...] = falling_order(count_ref[...])
    low, high, far = at(3), at(1), at(2)
    forwards = {0: pass_on(low, 0, 2, up), 3: pass_on(high, 1, 5, down)}
    shares = {0: (low, 0, 8), 3: (high, 1, 9), 1: (low, 1, 10), 4: (high, 0, 11), 2: (far, 0, 12), 5: (far, 1, 13)}
    ring = {index: own(0, index, up) for index in (0, 1, 2, 3, 4, 5)}
    near = {index: own(0, index, other) for index in range(6, 14)}

    def arrive(index):
        ring[index].wait_recv()
        source, h, share = shares[index]
        for copy in [forwards[index]] if index in forwards else []:
            copy.start()
            sent.append(copy)
        sent.append(pass_on(source, h, share, other))
        sent[-1].start()
        project_half(source, h)

    def arrive_near(share, source, h):
        near[share].wait_recv()
        project_half(source, h)

    arrive_near(6, at(0, 1), 0)
    arrive_near(7, at(0, 1), 1)
    arrive(0)
    arrive(3)
    arrive_near(8, at(3, 1), 0)
    arrive_near(9, at(1, 1), 1)
    arrive(1)
    arrive(4)
    arrive_near(10, at(3, 1), 1)
    arrive_near(11, at(1, 1), 0)
    arrive(2)
    arrive(5)
    arrive_near(12, at(2, 1), 0)
    arrive_near(13, at(2, 1), 1)
    for copy in given:
        copy.wait_recv()
    for copy in sent + given:
        copy.wait_send()
    for store in stores:
        store.wait()


def project(x, g, wi, wo, counts):
    nodes, width = x.shape
    span = nodes * H
    vm = pl.BlockSpec(memory_space=pltpu.VMEM)
    anywhere = pl.BlockSpec(memory_space=pl.ANY)
    cols = jax.ShapeDtypeStruct((2 * HD, span), BF16)
    return pl.pallas_call(
        project_kernel,
        out_shape=(
            jax.ShapeDtypeStruct((span, 2 * HD), BF16),
            cols,
            cols,
            jax.ShapeDtypeStruct(counts.shape, jnp.int32),
            jax.ShapeDtypeStruct((span, width), BF16),
        ),
        in_specs=[anywhere] * 4 + [vm],
        out_specs=(vm,) * 4 + (anywhere,),
        scratch_shapes=[
            pltpu.VMEM((H, nodes, width), BF16),
            pltpu.VMEM(g.shape, BF16),
            pltpu.VMEM(wi.shape, BF16),
            pltpu.VMEM(wo.shape, BF16),
            pltpu.VMEM((width, nodes), BF16),
            pltpu.SemaphoreType.DMA((21,)),
            pltpu.SemaphoreType.DMA((21,)),
            pltpu.SemaphoreType.DMA((4,)),
            pltpu.SemaphoreType.DMA((2 * H,)),
        ],
        compiler_params=pltpu.CompilerParams(collective_id=0, has_side_effects=True, vmem_limit_bytes=VMEM_BYTES),
        name="project",
    )(x, g, wi, wo, counts)


def attention_kernel(
    group, order_ref, blocks_ref, counts_ref, kv_ref, kvt_ref, qgt_ref, all_hbm, grads_ref, weight_ref,
    total_ref, all_ref, load_sem,
):
    block_count = kvt_ref.shape[1] // B
    load = pltpu.make_async_copy(all_hbm, all_ref, load_sem)
    load.start()
    total_ref[...] = jnp.zeros_like(total_ref)
    zero = jnp.zeros((HD, B), BF16)

    def query_blocks(ids, live):
        heres = [pl.ds(pl.multiple_of(i * B, B), B) for i in ids]
        spots = [[pl.ds(pl.multiple_of(blocks_ref[i, j] * B, B), B) for j in range(live)] for i in ids]
        aparts, products = [], []
        for here, chosen in zip(heres, spots):
            qgt = qgt_ref[:, here]
            apart = jnp.concatenate(
                [jnp.concatenate([qgt[:HD], zero], 1), jnp.concatenate([zero, qgt[HD:]], 1)], 0
            )
            aparts.append(apart)
            products.append(dot(jnp.concatenate([kv_ref[spot, :] for spot in chosen], 0), apart))
        pairs = []
        for i, product in zip(ids, products):
            count = counts_ref[i]
            scores = [product[:B, :B]]
            for j in range(1, live):
                scores.append(product[j * B : (j + 1) * B, :B] + jnp.where(j < count, 0.0, NEGATIVE))
            scores = jnp.concatenate(scores, 0)
            grad_probs = product[:, B:]
            raised = jnp.exp(scores - jnp.max(scores, 0, keepdims=True))
            inverse = 1.0 / jnp.sum(raised, 0, keepdims=True)
            row_delta = jnp.sum(raised * grad_probs, 0, keepdims=True) * inverse
            probs = raised * inverse
            grad_scores = (probs * (grad_probs - row_delta)).astype(BF16)
            pairs.append(jnp.concatenate([grad_scores, probs.astype(BF16)], 1))
        outs = []
        for chosen, pair in zip(spots, pairs):
            outs.append(dot(jnp.concatenate([kvt_ref[:, spot] for spot in chosen], 1), pair))
        terms = []
        for apart, pair in zip(aparts, pairs):
            terms.append(dot(apart, pair, NT))
        for here, out in zip(heres, outs):
            grads_ref[0:HD, here] = out[HD:, B:].astype(BF16)
            grads_ref[HD : 2 * HD, here] = (out[:HD, :B] * SCALE).astype(BF16)
        for chosen, term in zip(spots, terms):
            for j, spot in enumerate(chosen):
                total_ref[:, spot] += term[:, j * B : (j + 1) * B]

    def step(index, carry):
        ids = [order_ref[0, index * group + t] for t in range(group)]
        most = counts_ref[ids[0]]
        for live in range(1, KMAX + 1):
            pl.when(most == live)(partial(query_blocks, ids, live))
        return carry

    lax.fori_loop(0, block_count // group, step, 0)
    grads_ref[2 * HD :, :] = total_ref[...].astype(BF16)
    load.wait()
    weight_ref[...] = dot(grads_ref[HD:, :], all_ref[...])


def attention(order, blocks, counts, kv, kvt, qgt, everything):
    span, width = everything.shape
    vm = pl.BlockSpec(memory_space=pltpu.VMEM)
    sm = pl.BlockSpec(memory_space=pltpu.SMEM)
    return pl.pallas_call(
        partial(attention_kernel, 4),
        out_shape=(jax.ShapeDtypeStruct((4 * HD, span), BF16), jax.ShapeDtypeStruct((3 * HD, width), F32)),
        in_specs=[sm, sm, sm, vm, vm, vm, pl.BlockSpec(memory_space=pl.ANY)],
        out_specs=(vm, vm),
        scratch_shapes=[
            pltpu.VMEM((2 * HD, span), F32),
            pltpu.VMEM(everything.shape, BF16),
            pltpu.SemaphoreType.DMA,
        ],
        compiler_params=pltpu.CompilerParams(vmem_limit_bytes=VMEM_BYTES),
        name="attention",
    )(order, blocks, counts, kv, kvt, qgt, everything)


ROWS = (256, 64, 16)


class Sum:
    def __init__(self, number, axes, columns, whole, sems, scratch, along, place_of, core):
        self.number, self.axes, self.columns, self.whole, self.sems = number, axes, columns, whole, sems
        self.total, self.out, self.quarters, self.parts, self.levels = scratch
        self.along = along
        self.place = [place_of[axis] for axis in axes]
        self.core = core
        self.waiting, self.sent = [], []

    def send(self, phase, axis, source, target):
        self.waiting = []
        for offset in (2, 1, 3):
            copy = remote(
                source(offset), target(offset), self.sems, (self.number, phase, offset - 1), self.along(axis, offset)
            )
            copy.start()
            self.waiting.append(copy)
        self.sent += self.waiting

    def arrive(self):
        for copy in self.waiting:
            copy.wait_recv()

    def scatter_first(self, value):
        self.total[...] = value
        self.out[0 : ROWS[0], :] = value.astype(BF16)
        spot = lambda offset: part((self.place[0] + offset) % SIDE, ROWS[1])
        self.send(
            0, self.axes[0], lambda o: self.out.at[spot(o), :], lambda o: self.quarters.at[o - 1]
        )

    def scatter_second(self):
        self.arrive()
        value = self.total[part(self.place[0], ROWS[1]), :] + self.quarters[0].astype(F32)
        value += self.quarters[1].astype(F32) + self.quarters[2].astype(F32)
        self.total[0 : ROWS[1], :] = value
        self.out[ROWS[0] :, :] = value.astype(BF16)
        spot = lambda offset: part(ROWS[0] // ROWS[2] + (self.place[1] + offset) % SIDE, ROWS[2])
        self.send(1, self.axes[1], lambda o: self.out.at[spot(o), :], lambda o: self.parts.at[o - 1])

    def scattered(self):
        self.arrive()
        value = self.total[part(self.place[1], ROWS[2]), :] + self.parts[0].astype(F32)
        return (value + (self.parts[1].astype(F32) + self.parts[2].astype(F32))).astype(BF16)

    def exchange(self, axis, place):
        self.levels[place] = self.scattered()
        here = self.levels.at[place]
        self.send(2, axis, lambda o: here, lambda o: here)

    def exchanged(self):
        self.arrive()
        value = [self.levels[k].astype(F32) for k in range(SIDE)]
        self.region(2)[...] = ((value[0] + value[1]) + (value[2] + value[3])).astype(BF16)

    def region(self, level, columns=None):
        first = self.core * ROWS[0]
        if level >= 1:
            first = first + self.place[0] * ROWS[1]
        if level >= 2:
            first = first + self.place[1] * ROWS[2]
        rows = pl.ds(pl.multiple_of(first, ROWS[2]), ROWS[level])
        return self.whole.at[rows, self.columns if columns is None else columns]

    def gather(self, step):
        here = self.region(2 - step)
        self.send(3 + step, self.axes[1 - step], lambda o: here, lambda o: here)


def finish_kernel(
    grads_hbm, weight_hbm, x_hbm, g_hbm, wi_hbm, wo_hbm,
    layer_ref, gradf_ref, osum_ref, isum_ref,
    x_ref, g_ref, wi_ref, wo_ref, attended_ref, rows_ref, merged_ref, theirs_ref, half_ref, total_ref,
    tot_a, tot_b, tot_c, tot_d, out_a, out_b, out_c, out_d, quarters_a, quarters_b, quarters_c, quarters_d,
    parts_a, parts_b, parts_c, parts_d, levels_c, levels_d,
    seq_send, seq_recv, core_send, core_recv, sum_send, sum_recv, spread_send, spread_recv, load_sem,
):
    dp, seq = lax.axis_index("dp"), lax.axis_index("seq")
    z, x, y, core = dp // SIDE, dp % SIDE, seq // 2, seq % 2
    place_of = {"x": x, "y": y, "z": z}
    nodes, width = x_ref.shape
    half = nodes // 2
    other = (dp, y * 2 + (core + 1) % 2)
    seq_sems, core_sems = (seq_send, seq_recv), (core_send, core_recv)

    def along(axis, offset):
        if axis == "y":
            return (dp, ((y + offset) % SIDE) * 2 + core)
        if axis == "x":
            return (z * SIDE + (x + offset) % SIDE, seq)
        return (((z + offset) % SIDE) * SIDE + x, seq)

    loads = [
        pltpu.make_async_copy(source, target, load_sem.at[k])
        for k, (source, target) in enumerate(
            (
                (x_hbm, x_ref),
                (g_hbm, g_ref),
                (wi_hbm, wi_ref),
                (wo_hbm, wo_ref),
                (weight_hbm.at[:, :, part(core, ROWS[0])], merged_ref.at[:, part(core, HD), :]),
                (grads_hbm.at[0, :, part(seq, nodes)], attended_ref.at[part(seq, HD), :]),
                (grads_hbm.at[pl.ds(1, 3), :, part(seq, nodes)], rows_ref.at[:, part(seq, HD), :]),
            )
        )
    ]
    for load in loads:
        load.start()
    peers = seq_peers(seq)
    greet([(dp, peer) for peer in peers] + [along(axis, offset) for axis in ("x", "z") for offset in (1, 2, 3)])

    sent = []

    def back(piece, source, target):
        copies = []
        for place, peer in enumerate(peers):
            copies.append(remote(source(peer), target, seq_sems, (piece, place), (dp, peer)))
            copies[-1].start()
        sent.extend(copies)
        return copies

    def back_rows(kind, h):
        mine = pl.ds(h * half, half)
        return back(
            1 + 2 * kind + h,
            lambda peer: grads_hbm.at[1 + kind, :, part(2 * peer + h, half)],
            rows_ref.at[kind, part(seq, HD), mine],
        )

    back_attended = back(0, lambda peer: grads_hbm.at[0, :, part(peer, nodes)], attended_ref.at[part(seq, HD), :])
    swap = remote(
        weight_hbm.at[:, :, part(1 - core, ROWS[0])], theirs_ref, core_sems, 0, other
    )
    swap.start()
    sent.append(swap)

    sums = (sum_send, sum_recv)
    make = lambda *args: Sum(*args, along, place_of, core)
    both = make(0, ("z", "x"), pl.ds(0, 2 * width), isum_ref, sums, (tot_a, out_a, quarters_a, parts_a, None))
    last = make(1, ("x", "z"), pl.ds(2 * width, width), isum_ref, sums, (tot_b, out_b, quarters_b, parts_b, None))
    left = make(2, ("x", "z"), pl.ds(0, half), osum_ref, sums, (tot_c, out_c, quarters_c, parts_c, levels_c))
    right = make(3, ("z", "x"), pl.ds(half, half), osum_ref, sums, (tot_d, out_d, quarters_d, parts_d, levels_d))

    loads[4].wait()
    swap.wait_recv()
    merged_ref[:, part(1 - core, HD), :] = theirs_ref[...]
    last.scatter_first(merged_ref[2].T)
    both.scatter_first(jnp.concatenate([merged_ref[0].T, merged_ref[1].T], 1))
    back_q = back_rows(0, 0)
    last.scatter_second()
    both.scatter_second()

    for load in loads[:4] + loads[5:]:
        load.wait()
    for copy in back_attended:
        copy.wait_recv()
    total_ref[...] = dot(attended_ref[...], g_ref[...])
    half_ref[0] = total_ref[part(1 - core, ROWS[0]), :].astype(BF16)
    merge = remote(half_ref.at[0], half_ref.at[1], core_sems, 1, other)
    merge.start()
    sent.append(merge)

    spread = []
    for job, kinds in ((last, (2,)), (both, (0, 1))):
        value = job.scattered()
        for k, kind in enumerate(kinds):
            columns = pl.ds(pl.multiple_of(kind * width + y * 2 * HD, 2 * HD), 2 * HD)
            here = job.region(2, columns)
            here[...] = value[:, k * 2 * HD : (k + 1) * 2 * HD]
            for offset in (2, 1, 3):
                spread.append(remote(here, here, (spread_send, spread_recv), (kind, offset - 1), along("y", offset)))
                spread[-1].start()
    sent.extend(spread)
    back_q += back_rows(0, 1)
    back_k = back_rows(1, 0)

    layer_ref[...] = (x_ref[...].astype(F32) + dot(attended_ref[...], wo_ref[...], TN)).astype(BF16)

    merge.wait_recv()
    merged = total_ref[part(core, ROWS[0]), :] + half_ref[1].astype(F32)
    left.scatter_first(merged[:, :half])
    right.scatter_first(merged[:, half:])
    for copy in spread:
        copy.wait_recv()
    last.gather(0)
    both.gather(0)
    left.scatter_second()
    right.scatter_second()
    left.exchange("y", y)
    right.exchange("y", y)
    back_k += back_rows(1, 1)
    back_v = back_rows(2, 0) + back_rows(2, 1)
    last.arrive()
    last.gather(1)
    both.arrive()
    both.gather(1)
    for copy in back_q:
        copy.wait_recv()
    total_ref[...] = dot(wi_ref[:, :width], rows_ref[0])
    left.exchanged()
    left.gather(0)
    right.exchanged()
    right.gather(0)
    for copy in back_k:
        copy.wait_recv()
    total_ref[...] += dot(wi_ref[:, width : 2 * width], rows_ref[1])
    left.arrive()
    left.gather(1)
    right.arrive()
    right.gather(1)
    last.arrive()
    both.arrive()

    def share(whole, index):
        mine = whole.at[part(core, ROWS[0]), :]
        copy = remote(mine, mine, core_sems, index, other)
        copy.start()
        sent.append(copy)
        return copy

    share_i = share(isum_ref, 2)
    for copy in back_v:
        copy.wait_recv()
    turned = (total_ref[...] + dot(wi_ref[:, 2 * width :], rows_ref[2])).T
    gradf_ref[...] = (g_ref[...].astype(F32) + turned).astype(BF16)
    left.arrive()
    right.arrive()
    share_o = share(osum_ref, 3)
    share_i.wait_recv()
    share_o.wait_recv()
    for job in (both, last, left, right):
        sent.extend(job.sent)
    for copy in sent:
        copy.wait_send()


def finish(grads, weight, x, g, wi, wo):
    nodes, width = x.shape
    vm = pl.BlockSpec(memory_space=pltpu.VMEM)
    anywhere = pl.BlockSpec(memory_space=pl.ANY)
    rows = jax.ShapeDtypeStruct((nodes, width), BF16)
    columns = (4 * HD, 2 * HD, width // 2, width // 2)
    dma = pltpu.SemaphoreType.DMA
    return pl.pallas_call(
        finish_kernel,
        out_shape=(
            rows,
            rows,
            jax.ShapeDtypeStruct((width, width), BF16),
            jax.ShapeDtypeStruct((width, 3 * width), BF16),
        ),
        in_specs=[anywhere] * 6,
        out_specs=(vm,) * 4,
        scratch_shapes=[
            pltpu.VMEM(x.shape, BF16),
            pltpu.VMEM(g.shape, BF16),
            pltpu.VMEM(wi.shape, BF16),
            pltpu.VMEM(wo.shape, BF16),
            pltpu.VMEM((width, nodes), BF16),
            pltpu.VMEM((3, width, nodes), BF16),
            pltpu.VMEM((3, 2 * HD, ROWS[0]), F32),
            pltpu.VMEM((3, HD, ROWS[0]), F32),
            pltpu.VMEM((2, ROWS[0], width), BF16),
            pltpu.VMEM((width, nodes), F32),
        ]
        + [pltpu.VMEM((ROWS[0], n), F32) for n in columns]
        + [pltpu.VMEM((ROWS[0] + ROWS[1], n), BF16) for n in columns]
        + [pltpu.VMEM((SIDE - 1, ROWS[1], n), BF16) for n in columns]
        + [pltpu.VMEM((SIDE - 1, ROWS[2], n), BF16) for n in columns]
        + [pltpu.VMEM((SIDE, ROWS[2], n), BF16) for n in columns[2:]]
        + [dma((7, H - 1))] * 2
        + [dma((4,))] * 2
        + [dma((4, 5, SIDE - 1))] * 2
        + [dma((3, SIDE - 1))] * 2
        + [dma((7,))],
        compiler_params=pltpu.CompilerParams(collective_id=1, has_side_effects=True, vmem_limit_bytes=VMEM_BYTES),
        name="finish",
    )(grads.reshape(4, HD, -1), weight.reshape(3, HD, -1), x, g, wi, wo)


def emit_kernel(factor, layer_ref, gradf_ref, osum_ref, isum_ref, layer_out, gradf_out, osum_out, isum_out):
    layer_out[...] = layer_ref[...]
    gradf_out[...] = gradf_ref[...]
    osum_out[...] = osum_ref[...].astype(F32) * factor
    isum_out[...] = isum_ref[...].astype(F32) * factor


def emit(layer, gradf, osum, isum, factor):
    arrays = (layer, gradf, osum, isum)
    kinds = (BF16, BF16, F32, F32)
    specs = [pl.BlockSpec((B, a.shape[1]), lambda i: (i, 0)) for a in arrays]
    return pl.pallas_call(
        partial(emit_kernel, factor),
        grid=(layer.shape[0] // B,),
        out_shape=tuple(jax.ShapeDtypeStruct(a.shape, kind) for a, kind in zip(arrays, kinds)),
        in_specs=specs,
        out_specs=tuple(specs),
        compiler_params=pltpu.CompilerParams(vmem_limit_bytes=VMEM_BYTES),
        name="emit",
    )(*arrays)


def shards(features, input_weight, output_weight, key_blocks, key_count, cotangent):
    x, g = features[0], cotangent[0]
    kv, kvt, qgt, order, everything = project(x, g, input_weight, output_weight, key_count[0])
    grads, weight = attention(order, key_blocks[0, 0], key_count[0, 0], kv, kvt, qgt, everything)
    results = finish(grads, weight, x, g, input_weight, output_weight)
    factor = 1.0 / (lax.axis_size("dp") * lax.axis_size("seq") * x.shape[0]) ** 0.5
    layer_out, grad_features, output_total, input_total = emit(*results, factor)
    return (layer_out[None], grad_features[None], input_total, output_total)


def solution(mesh):
    in_specs = (
        P("dp", "seq", None),
        P(),
        P(),
        P("dp", "seq", None, None),
        P("dp", "seq", None),
        P("dp", "seq", None),
    )
    out_specs = (P("dp", "seq", None), P("dp", "seq", None), P(), P())
    return jax.shard_map(shards, mesh=mesh, in_specs=in_specs, out_specs=out_specs, check_vma=False)
```

time: 679 us -> 99.7 us (0.15)
  waiting for transfers between devices: 198 us -> 0 us
  local copies, waits for them, and re-layouts: 167 us -> 1.37 us
  other arithmetic: 134 us -> 0 us
  matrix products: 128 us -> 0 us
  Pallas kernels: 0 us -> 97.4 us
  starting transfers between devices: 20.8 us -> 0 us
  between operations: 14.2 us -> 0.66 us
  loops' own time: 11.9 us -> 0 us
    psum x1 -> x0, waiting for transfers between devices: 150 us -> none  [shards(): lax.psum((input_terms, output_terms), ('dp', 'seq'))]
    dot_general x62 -> x0, matrix products: 128 us -> none  [the longest x16 41.2 us: block_probs(): jnp.einsum('eqr,eqjc->qrjc', queries, key_tiles, preferred_element_type=j...]
    pallas_call x0 -> x4, Pallas kernels: none -> 97.4 us  [the longest x1 40.1 us: finish(): pl.pallas_call(finish_kernel, out_shape=(rows, rows, jax.ShapeDtypeStruct...]
    scatter-add x24 -> x0, other arithmetic: 81.8 us -> none  [the longest x8 43.5 us: advance(): grad_values.at[:, chosen]]
    all_to_all x4 -> x0, waiting for transfers between devices: 47.2 us -> none  [the longest x1 24.3 us: shards(): lax.all_to_all(proj_cols, 'seq', split_axis=1, concat_axis=2, tiled=True)]
    gather x64 -> x0, local copies, waits for them, and re-layouts: 46.4 us -> none  [the longest x24 12 us: advance(): key_tiles = jnp.take(keys_all, chosen, axis=1)]
    while x108 -> x0, local copies, waits for them, and re-layouts: 30.9 us -> none  [the longest x8 18.3 us: advance(): lax.dynamic_slice_in_dim(grad_attended, first_block, per_step, 1)]
    another operation x24 -> x0, local copies, waits for them, and re-layouts: 21.3 us -> none
  transfers between devices with their start and end apart: 5 -> 0, of which waited for: 4 -> 0; matrix products, arithmetic and copies ran while one was open for 4% -> 0% of each run, Pallas kernels for 0% -> 0%
where the time goes in v3:
time: 99.7 us; the launch traced here: 99.4 us
  Pallas kernels  97.4 us (98%)
  local copies, waits for them, and re-layouts  1.37 us (1%)
    pallas_call x1, Pallas kernels, finish(): pl.pallas_call(finish_kernel, out_shape=(rows, rows, jax.ShapeDtypeStruct...  40.1 us
    pallas_call x1, Pallas kernels, project(): pl.pallas_call(project_kernel, out_shape=(jax.ShapeDtypeStruct((span, 2 *...  34.4 us
    pallas_call x1, Pallas kernels, attention(): pl.pallas_call(partial(attention_kernel, 4), out_shape=(jax.ShapeDtypeStr...  18.1 us
    pallas_call x1, Pallas kernels, emit(): pl.pallas_call(partial(emit_kernel, factor), grid=(layer.shape[0] // B,),...  4.75 us

profile of v3, /device:TPU:1, one launch (start us, length us, event | category | flops | bytes accessed | tf_op | source)
XLA Modules:
  0.0 99.4 jit_solution(7333625128416878242)
XLA Ops:
  0.6 1.4 %copy.10 = s32[1,1,32,8]{3,2,1,0:T(8,128)} copy(s32[1,1,32,8]{2,3,1,0:T(8,128)} %param.9) | data formatting | bytes 2048 | tf_op args[3]
  2.0 34.4 %project.1 = (bf16[4096,128]{1,0:T(8,128)(2,1)}, bf16[128,4096]{1,0:T(8,128)(2,1)}, bf16[128,4096]{1,0:T(8,128)(2,1)}, s32[1,32]{1,0:T(1,128)}, bf16[4096,512]{1,0:T(8,128)(2,1)}) custom-call(bf16[512,512]{1,0:T(8,128)(2,1)} %bitcast.10, bf16[512,512]{1,0:T(8,128)(2,1)} %bitcast.12, bf16[512,1536]{1,0:T(8,128)(2,1)} %wi_hbm.3, bf16[512,512]{1,0:T(8,128)(2,1)} %wo_hbm.3, ...), custom_call_target="tpu_custom_call" | custom-call | tf_op jit(solution)/shard_map/project/pallas_call | solution.py:199
  36.4 18.1 %attention.1 = (bf16[256,4096]{1,0:T(8,128)(2,1)}, f32[192,512]{1,0:T(8,128)}) custom-call(s32[1,32]{1,0:T(1,128)} %get-tuple-element.19.order_ref, s32[32,8]{1,0:T(8,128)} %bitcast.15, s32[32]{0:T(128)} %bitcast.17, bf16[4096,128]{1,0:T(8,128)(2,1)} %get-tuple-element.20.kv_ref, bf16[128,4096]{1,0:T(8,128)(2,1)} %get-tuple-element.21.kvt_ref, ...), custom_call_target="tpu_custom_call" | custom-call | tf_op jit(solution)/shard_map/attention/pallas_call | solution.py:291
  54.5 40.1 %finish.1 = (bf16[512,512]{1,0:T(8,128)(2,1)}, bf16[512,512]{1,0:T(8,128)(2,1)}, bf16[512,512]{1,0:T(8,128)(2,1)}, bf16[512,1536]{1,0:T(8,128)(2,1)}) custom-call(bf16[4,64,4096]{2,1,0:T(8,128)(2,1)} %bitcast.9, f32[3,64,512]{2,1,0:T(8,128)} %bitcast.14, bf16[512,512]{1,0:T(8,128)(2,1)} %bitcast.11, bf16[512,512]{1,0:T(8,128)(2,1)} %bitcast.13, ...), custom_call_target="tpu_custom_call" | custom-call | tf_op jit(solution)/shard_map/finish/pallas_call | solution.py:552
  94.7 4.7 %emit.1 = (bf16[512,512]{1,0:T(8,128)(2,1)}, bf16[512,512]{1,0:T(8,128)(2,1)}, f32[512,512]{1,0:T(8,128)}, f32[512,1536]{1,0:T(8,128)}) custom-call(bf16[512,512]{1,0:T(8,128)(2,1)} %get-tuple-element.26.layer_ref, bf16[512,512]{1,0:T(8,128)(2,1)} %get-tuple-element.27.gradf_ref, bf16[512,512]{1,0:T(8,128)(2,1)} %get-tuple-element.28.osum_ref, ...), custom_call_target="tpu_custom_call" | custom-call | tf_op jit(solution)/shard_map/emit/pallas_call | solution.py:600

commit v4 on v3

--- a/solution.py
+++ b/solution.py
@@ -73,8 +73,8 @@
 
 def project_kernel(
     x_hbm, g_hbm, wi_hbm, wo_hbm, count_ref,
-    kv_ref, kvt_ref, qgt_ref, order_ref, all_hbm,
-    x_ref, g_ref, wi_ref, wo_ref, gt_ref, send_sem, recv_sem, load_sem, store_sem,
+    order_ref, all_hbm, kv_hbm, kvt_hbm, qt_hbm, gt_hbm,
+    x_ref, kv_ref, kvt_ref, qt_ref, g_ref, wi_ref, wo_ref, grad_ref, send_sem, recv_sem, load_sem, store_sem,
 ):
     dp, seq = lax.axis_index("dp"), lax.axis_index("seq")
     y, core = seq // 2, seq % 2
@@ -86,15 +86,15 @@
     def at(dy, flip=0):
         return ((y + dy) % SIDE) * 2 + (core + flip) % 2
 
+    peers = seq_peers(seq)
     loads = [
         pltpu.make_async_copy(source, target, load_sem.at[k])
         for k, (source, target) in enumerate(
-            ((x_hbm, x_ref.at[seq]), (g_hbm, g_ref), (wi_hbm, wi_ref), (wo_hbm, wo_ref))
+            ((x_hbm, x_ref.at[seq]), (wi_hbm, wi_ref), (g_hbm, g_ref), (wo_hbm, wo_ref))
         )
     ]
     for load in loads:
         load.start()
-    peers = seq_peers(seq)
     greet([(dp, peer) for peer in peers])
     up, down = (dp, at(1)), (dp, at(3))
 
@@ -112,19 +112,8 @@
     for copy in sent:
         copy.start()
 
+    loads[0].wait()
     loads[1].wait()
-    loads[3].wait()
-    gt_ref[...] = dot(wo_ref[...], g_ref[...], NT).astype(BF16)
-    head_rows = pl.ds(HD, HD)
-    given = []
-    for place, peer in enumerate(peers):
-        given.append(
-            remote(gt_ref.at[part(peer, HD), :], qgt_ref.at[head_rows, part(seq, nodes)], sems, 14 + place, (dp, peer))
-        )
-        given[-1].start()
-    qgt_ref[head_rows, part(seq, nodes)] = gt_ref[part(seq, HD), :]
-    loads[2].wait()
-    loads[0].wait()
     chosen = []
     for kind in (1, 2, 0):
         block = wi_ref[:, pl.ds(pl.multiple_of(kind * width + y * 2 * HD, 2 * HD), 2 * HD)]
@@ -133,20 +122,28 @@
     weights = jnp.concatenate(chosen + [jnp.zeros_like(chosen[0])], 1)
     stores = []
 
+    def store(source, target):
+        stores.append(pltpu.make_async_copy(source, target, store_sem.at[len(stores)]))
+        stores[-1].start()
+
     def project_half(source, h):
-        place = 2 * source + h
-        here = part(place, half)
+        here = part(2 * source + h, half)
         product = dot(x_ref[source, rows(h), :], weights)
         kv = product[:, : 2 * HD].astype(BF16)
         kv_ref[here, :] = kv
         kvt_ref[:, here] = kv.T
-        qgt_ref[:HD, here] = product[:, 2 * HD :].T[:HD].astype(BF16)
-        store = pltpu.make_async_copy(x_ref.at[source, rows(h)], all_hbm.at[here, :], store_sem.at[len(stores)])
-        store.start()
-        stores.append(store)
+        qt_ref[:, here] = product[:, 2 * HD :].T[:HD].astype(BF16)
+        store(x_ref.at[source, rows(h)], all_hbm.at[here, :])
+        store(kv_ref.at[here, :], kv_hbm.at[here, :])
+        store(kvt_ref.at[:, here], kvt_hbm.at[:, here])
+        store(qt_ref.at[:, here], qt_hbm.at[:, here])
 
     project_half(seq, 0)
     project_half(seq, 1)
+    loads[2].wait()
+    loads[3].wait()
+    grad_ref[...] = dot(wo_ref[...], g_ref[...], NT).astype(BF16)
+    store(grad_ref.at[part(seq, HD), :], gt_hbm.at[:, part(seq, nodes)])
     order_ref[...] = falling_order(count_ref[...])
     low, high, far = at(3), at(1), at(2)
     forwards = {0: pass_on(low, 0, 2, up), 3: pass_on(high, 1, 5, down)}
@@ -162,7 +159,9 @@
             sent.append(copy)
         sent.append(pass_on(source, h, share, other))
         sent[-1].start()
-        project_half(source, h)
+
+    def project_arrived(index):
+        project_half(*shares[index][:2])
 
     def arrive_near(share, source, h):
         near[share].wait_recv()
@@ -172,22 +171,34 @@
     arrive_near(7, at(0, 1), 1)
     arrive(0)
     arrive(3)
+    given = []
+    for place, peer in enumerate(peers):
+        given.append(
+            remote(grad_ref.at[part(peer, HD), :], gt_hbm.at[:, part(seq, nodes)], sems, 14 + place, (dp, peer))
+        )
+        given[-1].start()
+    project_arrived(0)
+    project_arrived(3)
     arrive_near(8, at(3, 1), 0)
     arrive_near(9, at(1, 1), 1)
     arrive(1)
     arrive(4)
+    project_arrived(1)
+    project_arrived(4)
     arrive_near(10, at(3, 1), 1)
     arrive_near(11, at(1, 1), 0)
     arrive(2)
     arrive(5)
+    project_arrived(2)
+    project_arrived(5)
     arrive_near(12, at(2, 1), 0)
     arrive_near(13, at(2, 1), 1)
     for copy in given:
         copy.wait_recv()
     for copy in sent + given:
         copy.wait_send()
-    for store in stores:
-        store.wait()
+    for copy in stores:
+        copy.wait()
 
 
 def project(x, g, wi, wo, counts):
@@ -195,28 +206,32 @@
     span = nodes * H
     vm = pl.BlockSpec(memory_space=pltpu.VMEM)
     anywhere = pl.BlockSpec(memory_space=pl.ANY)
-    cols = jax.ShapeDtypeStruct((2 * HD, span), BF16)
+    dma = pltpu.SemaphoreType.DMA
     return pl.pallas_call(
         project_kernel,
         out_shape=(
-            jax.ShapeDtypeStruct((span, 2 * HD), BF16),
-            cols,
-            cols,
             jax.ShapeDtypeStruct(counts.shape, jnp.int32),
             jax.ShapeDtypeStruct((span, width), BF16),
+            jax.ShapeDtypeStruct((span, 2 * HD), BF16),
+            jax.ShapeDtypeStruct((2 * HD, span), BF16),
+            jax.ShapeDtypeStruct((HD, span), BF16),
+            jax.ShapeDtypeStruct((HD, span), BF16),
         ),
         in_specs=[anywhere] * 4 + [vm],
-        out_specs=(vm,) * 4 + (anywhere,),
+        out_specs=(vm,) + (anywhere,) * 5,
         scratch_shapes=[
             pltpu.VMEM((H, nodes, width), BF16),
+            pltpu.VMEM((span, 2 * HD), BF16),
+            pltpu.VMEM((2 * HD, span), BF16),
+            pltpu.VMEM((HD, span), BF16),
             pltpu.VMEM(g.shape, BF16),
             pltpu.VMEM(wi.shape, BF16),
             pltpu.VMEM(wo.shape, BF16),
             pltpu.VMEM((width, nodes), BF16),
-            pltpu.SemaphoreType.DMA((21,)),
-            pltpu.SemaphoreType.DMA((21,)),
-            pltpu.SemaphoreType.DMA((4,)),
-            pltpu.SemaphoreType.DMA((2 * H,)),
+            dma((21,)),
+            dma((21,)),
+            dma((4,)),
+            dma((8 * H + 1,)),
         ],
         compiler_params=pltpu.CompilerParams(collective_id=0, has_side_effects=True, vmem_limit_bytes=VMEM_BYTES),
         name="project",
@@ -224,7 +239,7 @@
 
 
 def attention_kernel(
-    group, order_ref, blocks_ref, counts_ref, kv_ref, kvt_ref, qgt_ref, all_hbm, grads_ref, weight_ref,
+    group, order_ref, blocks_ref, counts_ref, kv_ref, kvt_ref, qt_ref, gt_ref, all_hbm, grads_ref, weight_ref,
     total_ref, all_ref, load_sem,
 ):
     block_count = kvt_ref.shape[1] // B
@@ -235,12 +250,11 @@
 
     def query_blocks(ids, live):
         heres = [pl.ds(pl.multiple_of(i * B, B), B) for i in ids]
-        spots = [[pl.ds(pl.multiple_of(blocks_ref[i, j] * B, B), B) for j in range(live)] for i in ids]
+        spots = [[pl.ds(pl.multiple_of(blocks_ref[j, i] * B, B), B) for j in range(live)] for i in ids]
         aparts, products = [], []
         for here, chosen in zip(heres, spots):
-            qgt = qgt_ref[:, here]
             apart = jnp.concatenate(
-                [jnp.concatenate([qgt[:HD], zero], 1), jnp.concatenate([zero, qgt[HD:]], 1)], 0
+                [jnp.concatenate([qt_ref[:, here], zero], 1), jnp.concatenate([zero, gt_ref[:, here]], 1)], 0
             )
             aparts.append(apart)
             products.append(dot(jnp.concatenate([kv_ref[spot, :] for spot in chosen], 0), apart))
@@ -258,11 +272,9 @@
             probs = raised * inverse
             grad_scores = (probs * (grad_probs - row_delta)).astype(BF16)
             pairs.append(jnp.concatenate([grad_scores, probs.astype(BF16)], 1))
-        outs = []
-        for chosen, pair in zip(spots, pairs):
+        outs, terms = [], []
+        for apart, chosen, pair in zip(aparts, spots, pairs):
             outs.append(dot(jnp.concatenate([kvt_ref[:, spot] for spot in chosen], 1), pair))
-        terms = []
-        for apart, pair in zip(aparts, pairs):
             terms.append(dot(apart, pair, NT))
         for here, out in zip(heres, outs):
             grads_ref[0:HD, here] = out[HD:, B:].astype(BF16)
@@ -284,14 +296,14 @@
     weight_ref[...] = dot(grads_ref[HD:, :], all_ref[...])
 
 
-def attention(order, blocks, counts, kv, kvt, qgt, everything):
+def attention(order, blocks, counts, kv, kvt, qt, gt, everything):
     span, width = everything.shape
     vm = pl.BlockSpec(memory_space=pltpu.VMEM)
     sm = pl.BlockSpec(memory_space=pltpu.SMEM)
     return pl.pallas_call(
         partial(attention_kernel, 4),
         out_shape=(jax.ShapeDtypeStruct((4 * HD, span), BF16), jax.ShapeDtypeStruct((3 * HD, width), F32)),
-        in_specs=[sm, sm, sm, vm, vm, vm, pl.BlockSpec(memory_space=pl.ANY)],
+        in_specs=[sm, sm, sm, vm, vm, vm, vm, pl.BlockSpec(memory_space=pl.ANY)],
         out_specs=(vm, vm),
         scratch_shapes=[
             pltpu.VMEM((2 * HD, span), F32),
@@ -300,7 +312,7 @@
         ],
         compiler_params=pltpu.CompilerParams(vmem_limit_bytes=VMEM_BYTES),
         name="attention",
-    )(order, blocks, counts, kv, kvt, qgt, everything)
+    )(order, blocks, counts, kv, kvt, qt, gt, everything)
 
 
 ROWS = (256, 64, 16)
@@ -596,10 +608,11 @@
 def emit(layer, gradf, osum, isum, factor):
     arrays = (layer, gradf, osum, isum)
     kinds = (BF16, BF16, F32, F32)
-    specs = [pl.BlockSpec((B, a.shape[1]), lambda i: (i, 0)) for a in arrays]
+    rows = layer.shape[0] // 2
+    specs = [pl.BlockSpec((rows, a.shape[1]), lambda i: (i, 0)) for a in arrays]
     return pl.pallas_call(
         partial(emit_kernel, factor),
-        grid=(layer.shape[0] // B,),
+        grid=(2,),
         out_shape=tuple(jax.ShapeDtypeStruct(a.shape, kind) for a, kind in zip(arrays, kinds)),
         in_specs=specs,
         out_specs=tuple(specs),
@@ -610,8 +623,8 @@
 
 def shards(features, input_weight, output_weight, key_blocks, key_count, cotangent):
     x, g = features[0], cotangent[0]
-    kv, kvt, qgt, order, everything = project(x, g, input_weight, output_weight, key_count[0])
-    grads, weight = attention(order, key_blocks[0, 0], key_count[0, 0], kv, kvt, qgt, everything)
+    order, everything, kv, kvt, qt, gt = project(x, g, input_weight, output_weight, key_count[0])
+    grads, weight = attention(order, key_blocks[0, 0].T, key_count[0, 0], kv, kvt, qt, gt, everything)
     results = finish(grads, weight, x, g, input_weight, output_weight)
     factor = 1.0 / (lax.axis_size("dp") * lax.axis_size("seq") * x.shape[0]) ** 0.5
     layer_out, grad_features, output_total, input_total = emit(*results, factor)

time: 99.7 us -> 93.8 us (0.941)
  Pallas kernels: 97.4 us -> 93 us
  local copies, waits for them, and re-layouts: 1.37 us -> 0 us
    pallas_call x1, Pallas kernels: 18.1 us -> 12.2 us  [attention(): pl.pallas_call(partial(attention_kernel, 4), out_shape=(jax.ShapeDtypeStr...]
    pallas_call x1, Pallas kernels: 40.1 us -> 45.4 us  [finish(): pl.pallas_call(finish_kernel, out_shape=(rows, rows, jax.ShapeDtypeStruct...]
    pallas_call x2, Pallas kernels: 39.1 us -> 35.4 us  [the longest x1 31.5 us: project(): pl.pallas_call(project_kernel, out_shape=(jax.ShapeDtypeStruct(counts.sha...]
    unnamed x1 -> x0, local copies, waits for them, and re-layouts: 1.37 us -> none
where the time goes in v4:
time: 93.8 us; the launch traced here: 93.6 us
  Pallas kernels  93 us (99%)
    pallas_call x1, Pallas kernels, finish(): pl.pallas_call(finish_kernel, out_shape=(rows, rows, jax.ShapeDtypeStruct...  45.4 us
    pallas_call x1, Pallas kernels, project(): pl.pallas_call(project_kernel, out_shape=(jax.ShapeDtypeStruct(counts.sha...  31.5 us
    pallas_call x1, Pallas kernels, attention(): pl.pallas_call(partial(attention_kernel, 4), out_shape=(jax.ShapeDtypeStr...  12.2 us
    pallas_call x1, Pallas kernels, emit(): pl.pallas_call(partial(emit_kernel, factor), grid=(2,), out_shape=tuple((...  3.85 us

profile of v4, /device:TPU:1, one launch (start us, length us, event | category | flops | bytes accessed | tf_op | source)
XLA Modules:
  0.0 93.6 jit_solution(11668271793782695035)
XLA Ops:
  0.6 31.5 %project.1 = (s32[1,32]{1,0:T(1,128)}, bf16[4096,512]{1,0:T(8,128)(2,1)}, bf16[4096,128]{1,0:T(8,128)(2,1)}, bf16[128,4096]{1,0:T(8,128)(2,1)}, bf16[64,4096]{1,0:T(8,128)(2,1)}, /*index=5*/bf16[64,4096]{1,0:T(8,128)(2,1)}) custom-call(bf16[512,512]{1,0:T(8,128)(2,1)} %bitcast.12, bf16[512,512]{1,0:T(8,128)(2,1)} %bitcast.14, bf16[512,1536]{1,0:T(8,128)(2,1)} %wi_hbm.3, ...), custom_call_target="tpu_custom_call" | custom-call | tf_op jit(solution)/shard_map/project/pallas_call | solution.py:210
  32.1 12.2 %attention.1 = (bf16[256,4096]{1,0:T(8,128)(2,1)}, f32[192,512]{1,0:T(8,128)}) custom-call(s32[1,32]{1,0:T(1,128)} %get-tuple-element.20.order_ref, s32[8,32]{1,0:T(8,128)} %bitcast.17, s32[32]{0:T(128)} %bitcast.19, bf16[4096,128]{1,0:T(8,128)(2,1)} %get-tuple-element.21.kv_ref, bf16[128,4096]{1,0:T(8,128)(2,1)} %get-tuple-element.22.kvt_ref, ...), custom_call_target="tpu_custom_call" | custom-call | tf_op jit(solution)/shard_map/attention/pallas_call | solution.py:303
  44.3 45.4 %finish.1 = (bf16[512,512]{1,0:T(8,128)(2,1)}, bf16[512,512]{1,0:T(8,128)(2,1)}, bf16[512,512]{1,0:T(8,128)(2,1)}, bf16[512,1536]{1,0:T(8,128)(2,1)}) custom-call(bf16[4,64,4096]{2,1,0:T(8,128)(2,1)} %bitcast.11, f32[3,64,512]{2,1,0:T(8,128)} %bitcast.16, bf16[512,512]{1,0:T(8,128)(2,1)} %bitcast.13, bf16[512,512]{1,0:T(8,128)(2,1)} %bitcast.15, ...), custom_call_target="tpu_custom_call" | custom-call | tf_op jit(solution)/shard_map/finish/pallas_call | solution.py:564
  89.8 3.9 %emit.1 = (bf16[512,512]{1,0:T(8,128)(2,1)}, bf16[512,512]{1,0:T(8,128)(2,1)}, f32[512,512]{1,0:T(8,128)}, f32[512,1536]{1,0:T(8,128)}) custom-call(bf16[512,512]{1,0:T(8,128)(2,1)} %get-tuple-element.28.layer_ref, bf16[512,512]{1,0:T(8,128)(2,1)} %get-tuple-element.29.gradf_ref, bf16[512,512]{1,0:T(8,128)(2,1)} %get-tuple-element.30.osum_ref, ...), custom_call_target="tpu_custom_call" | custom-call | tf_op jit(solution)/shard_map/emit/pallas_call | solution.py:613

commit v5 on v4

--- a/solution.py
+++ b/solution.py
@@ -193,12 +193,14 @@
     project_arrived(5)
     arrive_near(12, at(2, 1), 0)
     arrive_near(13, at(2, 1), 1)
-    for copy in given:
-        copy.wait_recv()
-    for copy in sent + given:
+    for copy in sent:
         copy.wait_send()
     for copy in stores:
         copy.wait()
+    for copy in given:
+        copy.wait_send()
+    for copy in given:
+        copy.wait_recv()
 
 
 def project(x, g, wi, wo, counts):
@@ -325,32 +327,31 @@
         self.along = along
         self.place = [place_of[axis] for axis in axes]
         self.core = core
-        self.waiting, self.sent = [], []
+        self.waiting, self.sent = {}, []
 
     def send(self, phase, axis, source, target):
-        self.waiting = []
+        copies = {}
         for offset in (2, 1, 3):
-            copy = remote(
+            copies[offset] = remote(
                 source(offset), target(offset), self.sems, (self.number, phase, offset - 1), self.along(axis, offset)
             )
-            copy.start()
-            self.waiting.append(copy)
-        self.sent += self.waiting
-
-    def arrive(self):
-        for copy in self.waiting:
-            copy.wait_recv()
+            copies[offset].start()
+        self.waiting[phase] = copies
+        self.sent += copies.values()
+
+    def arrive(self, *phases):
+        for phase in phases:
+            for copy in self.waiting[phase].values():
+                copy.wait_recv()
 
     def scatter_first(self, value):
         self.total[...] = value
         self.out[0 : ROWS[0], :] = value.astype(BF16)
         spot = lambda offset: part((self.place[0] + offset) % SIDE, ROWS[1])
-        self.send(
-            0, self.axes[0], lambda o: self.out.at[spot(o), :], lambda o: self.quarters.at[o - 1]
-        )
+        self.send(0, self.axes[0], lambda o: self.out.at[spot(o), :], lambda o: self.quarters.at[o - 1])
 
     def scatter_second(self):
-        self.arrive()
+        self.arrive(0)
         value = self.total[part(self.place[0], ROWS[1]), :] + self.quarters[0].astype(F32)
         value += self.quarters[1].astype(F32) + self.quarters[2].astype(F32)
         self.total[0 : ROWS[1], :] = value
@@ -359,7 +360,7 @@
         self.send(1, self.axes[1], lambda o: self.out.at[spot(o), :], lambda o: self.parts.at[o - 1])
 
     def scattered(self):
-        self.arrive()
+        self.arrive(1)
         value = self.total[part(self.place[1], ROWS[2]), :] + self.parts[0].astype(F32)
         return (value + (self.parts[1].astype(F32) + self.parts[2].astype(F32))).astype(BF16)
 
@@ -369,31 +370,39 @@
         self.send(2, axis, lambda o: here, lambda o: here)
 
     def exchanged(self):
-        self.arrive()
+        self.arrive(2)
         value = [self.levels[k].astype(F32) for k in range(SIDE)]
-        self.region(2)[...] = ((value[0] + value[1]) + (value[2] + value[3])).astype(BF16)
-
-    def region(self, level, columns=None):
-        first = self.core * ROWS[0]
-        if level >= 1:
-            first = first + self.place[0] * ROWS[1]
-        if level >= 2:
-            first = first + self.place[1] * ROWS[2]
-        rows = pl.ds(pl.multiple_of(first, ROWS[2]), ROWS[level])
+        self.region()[...] = ((value[0] + value[1]) + (value[2] + value[3])).astype(BF16)
+
+    def region(self, second=None, columns=None):
+        second = self.place[1] if second is None else second
+        first = self.core * ROWS[0] + self.place[0] * ROWS[1] + second * ROWS[2]
+        rows = pl.ds(pl.multiple_of(first, ROWS[2]), ROWS[2])
         return self.whole.at[rows, self.columns if columns is None else columns]
 
-    def gather(self, step):
-        here = self.region(2 - step)
-        self.send(3 + step, self.axes[1 - step], lambda o: here, lambda o: here)
+    def gather(self):
+        here = self.region()
+        self.send(3, self.axes[1], lambda o: here, lambda o: here)
+        self.send(4, self.axes[0], lambda o: here, lambda o: here)
+
+    def gather_on(self):
+        for offset, copy in self.waiting[3].items():
+            copy.wait_recv()
+            here = self.region((self.place[1] + SIDE - offset) % SIDE)
+            self.send(4 + offset, self.axes[0], lambda o: here, lambda o: here)
+
+    def gathered(self):
+        self.arrive(4, 5, 6, 7)
 
 
 def finish_kernel(
     grads_hbm, weight_hbm, x_hbm, g_hbm, wi_hbm, wo_hbm,
+    layer_hbm, gradf_hbm, osum_hbm, isum_hbm,
     layer_ref, gradf_ref, osum_ref, isum_ref,
     x_ref, g_ref, wi_ref, wo_ref, attended_ref, rows_ref, merged_ref, theirs_ref, half_ref, total_ref,
     tot_a, tot_b, tot_c, tot_d, out_a, out_b, out_c, out_d, quarters_a, quarters_b, quarters_c, quarters_d,
     parts_a, parts_b, parts_c, parts_d, levels_c, levels_d,
-    seq_send, seq_recv, core_send, core_recv, sum_send, sum_recv, spread_send, spread_recv, load_sem,
+    seq_send, seq_recv, core_send, core_recv, sum_send, sum_recv, spread_send, spread_recv, load_sem, store_sem,
 ):
     dp, seq = lax.axis_index("dp"), lax.axis_index("seq")
     z, x, y, core = dp // SIDE, dp % SIDE, seq // 2, seq % 2
@@ -414,12 +423,12 @@
         pltpu.make_async_copy(source, target, load_sem.at[k])
         for k, (source, target) in enumerate(
             (
-                (x_hbm, x_ref),
-                (g_hbm, g_ref),
-                (wi_hbm, wi_ref),
-                (wo_hbm, wo_ref),
                 (weight_hbm.at[:, :, part(core, ROWS[0])], merged_ref.at[:, part(core, HD), :]),
                 (grads_hbm.at[0, :, part(seq, nodes)], attended_ref.at[part(seq, HD), :]),
+                (g_hbm, g_ref),
+                (x_hbm, x_ref),
+                (wo_hbm, wo_ref),
+                (wi_hbm, wi_ref),
                 (grads_hbm.at[pl.ds(1, 3), :, part(seq, nodes)], rows_ref.at[:, part(seq, HD), :]),
             )
         )
@@ -429,7 +438,11 @@
     peers = seq_peers(seq)
     greet([(dp, peer) for peer in peers] + [along(axis, offset) for axis in ("x", "z") for offset in (1, 2, 3)])
 
-    sent = []
+    sent, stores = [], []
+
+    def store(source, target):
+        stores.append(pltpu.make_async_copy(source, target, store_sem.at[len(stores)]))
+        stores[-1].start()
 
     def back(piece, source, target):
         copies = []
@@ -447,12 +460,10 @@
             rows_ref.at[kind, part(seq, HD), mine],
         )
 
-    back_attended = back(0, lambda peer: grads_hbm.at[0, :, part(peer, nodes)], attended_ref.at[part(seq, HD), :])
-    swap = remote(
-        weight_hbm.at[:, :, part(1 - core, ROWS[0])], theirs_ref, core_sems, 0, other
-    )
+    swap = remote(weight_hbm.at[:, :, part(1 - core, ROWS[0])], theirs_ref, core_sems, 0, other)
     swap.start()
     sent.append(swap)
+    back_attended = back(0, lambda peer: grads_hbm.at[0, :, part(peer, nodes)], attended_ref.at[part(seq, HD), :])
 
     sums = (sum_send, sum_recv)
     make = lambda *args: Sum(*args, along, place_of, core)
@@ -461,17 +472,17 @@
     left = make(2, ("x", "z"), pl.ds(0, half), osum_ref, sums, (tot_c, out_c, quarters_c, parts_c, levels_c))
     right = make(3, ("z", "x"), pl.ds(half, half), osum_ref, sums, (tot_d, out_d, quarters_d, parts_d, levels_d))
 
-    loads[4].wait()
+    loads[0].wait()
     swap.wait_recv()
     merged_ref[:, part(1 - core, HD), :] = theirs_ref[...]
+    both.scatter_first(jnp.concatenate([merged_ref[0].T, merged_ref[1].T], 1))
     last.scatter_first(merged_ref[2].T)
-    both.scatter_first(jnp.concatenate([merged_ref[0].T, merged_ref[1].T], 1))
     back_q = back_rows(0, 0)
+    for load in loads[1:]:
+        load.wait()
+    both.scatter_second()
     last.scatter_second()
-    both.scatter_second()
-
-    for load in loads[:4] + loads[5:]:
-        load.wait()
+
     for copy in back_attended:
         copy.wait_recv()
     total_ref[...] = dot(attended_ref[...], g_ref[...])
@@ -481,11 +492,11 @@
     sent.append(merge)
 
     spread = []
-    for job, kinds in ((last, (2,)), (both, (0, 1))):
+    for job, kinds in ((both, (0, 1)), (last, (2,))):
         value = job.scattered()
         for k, kind in enumerate(kinds):
             columns = pl.ds(pl.multiple_of(kind * width + y * 2 * HD, 2 * HD), 2 * HD)
-            here = job.region(2, columns)
+            here = job.region(columns=columns)
             here[...] = value[:, k * 2 * HD : (k + 1) * 2 * HD]
             for offset in (2, 1, 3):
                 spread.append(remote(here, here, (spread_send, spread_recv), (kind, offset - 1), along("y", offset)))
@@ -493,85 +504,83 @@
     sent.extend(spread)
     back_q += back_rows(0, 1)
     back_k = back_rows(1, 0)
-
-    layer_ref[...] = (x_ref[...].astype(F32) + dot(attended_ref[...], wo_ref[...], TN)).astype(BF16)
-
     merge.wait_recv()
     merged = total_ref[part(core, ROWS[0]), :] + half_ref[1].astype(F32)
     left.scatter_first(merged[:, :half])
     right.scatter_first(merged[:, half:])
+    back_k += back_rows(1, 1)
+
+    layer_ref[...] = (x_ref[...].astype(F32) + dot(attended_ref[...], wo_ref[...], TN)).astype(BF16)
+    store(layer_ref, layer_hbm)
     for copy in spread:
         copy.wait_recv()
-    last.gather(0)
-    both.gather(0)
+    both.gather()
+    last.gather()
     left.scatter_second()
     right.scatter_second()
+    both.gather_on()
+    last.gather_on()
     left.exchange("y", y)
     right.exchange("y", y)
-    back_k += back_rows(1, 1)
     back_v = back_rows(2, 0) + back_rows(2, 1)
-    last.arrive()
-    last.gather(1)
-    both.arrive()
-    both.gather(1)
     for copy in back_q:
         copy.wait_recv()
     total_ref[...] = dot(wi_ref[:, :width], rows_ref[0])
     left.exchanged()
-    left.gather(0)
     right.exchanged()
-    right.gather(0)
+    left.gather()
+    right.gather()
+    both.gathered()
+    last.gathered()
+
+    def share(source, target, index):
+        mine = part(core, ROWS[0])
+        copy = remote(source.at[mine, :], target.at[mine, :], core_sems, index, other)
+        copy.start()
+        store(source.at[mine, :], target.at[mine, :])
+        sent.append(copy)
+        return copy
+
+    share_i = share(isum_ref, isum_hbm, 2)
+    left.gather_on()
+    right.gather_on()
     for copy in back_k:
         copy.wait_recv()
     total_ref[...] += dot(wi_ref[:, width : 2 * width], rows_ref[1])
-    left.arrive()
-    left.gather(1)
-    right.arrive()
-    right.gather(1)
-    last.arrive()
-    both.arrive()
-
-    def share(whole, index):
-        mine = whole.at[part(core, ROWS[0]), :]
-        copy = remote(mine, mine, core_sems, index, other)
-        copy.start()
-        sent.append(copy)
-        return copy
-
-    share_i = share(isum_ref, 2)
+    late = {id(copy) for copy in back_v}
+    settled = [copy for copy in sent if id(copy) not in late]
+    for job in (both, last, left, right):
+        settled.extend(job.sent)
+    for copy in settled + back_v:
+        copy.wait_send()
     for copy in back_v:
         copy.wait_recv()
     turned = (total_ref[...] + dot(wi_ref[:, 2 * width :], rows_ref[2])).T
     gradf_ref[...] = (g_ref[...].astype(F32) + turned).astype(BF16)
-    left.arrive()
-    right.arrive()
-    share_o = share(osum_ref, 3)
+    store(gradf_ref, gradf_hbm)
+    left.gathered()
+    right.gathered()
+    share_o = share(osum_ref, osum_hbm, 3)
+    share_o.wait_send()
+    for copy in stores:
+        copy.wait()
     share_i.wait_recv()
     share_o.wait_recv()
-    for job in (both, last, left, right):
-        sent.extend(job.sent)
-    for copy in sent:
-        copy.wait_send()
 
 
 def finish(grads, weight, x, g, wi, wo):
     nodes, width = x.shape
-    vm = pl.BlockSpec(memory_space=pltpu.VMEM)
     anywhere = pl.BlockSpec(memory_space=pl.ANY)
-    rows = jax.ShapeDtypeStruct((nodes, width), BF16)
     columns = (4 * HD, 2 * HD, width // 2, width // 2)
     dma = pltpu.SemaphoreType.DMA
+    results = [(nodes, width), (nodes, width), (width, width), (width, 3 * width)]
     return pl.pallas_call(
         finish_kernel,
-        out_shape=(
-            rows,
-            rows,
-            jax.ShapeDtypeStruct((width, width), BF16),
-            jax.ShapeDtypeStruct((width, 3 * width), BF16),
-        ),
+        out_shape=tuple(jax.ShapeDtypeStruct(shape, BF16) for shape in results),
         in_specs=[anywhere] * 6,
-        out_specs=(vm,) * 4,
-        scratch_shapes=[
+        out_specs=(anywhere,) * 4,
+        scratch_shapes=[pltpu.VMEM(shape, BF16) for shape in results]
+        + [
             pltpu.VMEM(x.shape, BF16),
             pltpu.VMEM(g.shape, BF16),
             pltpu.VMEM(wi.shape, BF16),
@@ -590,9 +599,9 @@
         + [pltpu.VMEM((SIDE, ROWS[2], n), BF16) for n in columns[2:]]
         + [dma((7, H - 1))] * 2
         + [dma((4,))] * 2
-        + [dma((4, 5, SIDE - 1))] * 2
+        + [dma((4, 8, SIDE - 1))] * 2
         + [dma((3, SIDE - 1))] * 2
-        + [dma((7,))],
+        + [dma((7,)), dma((4,))],
         compiler_params=pltpu.CompilerParams(collective_id=1, has_side_effects=True, vmem_limit_bytes=VMEM_BYTES),
         name="finish",
     )(grads.reshape(4, HD, -1), weight.reshape(3, HD, -1), x, g, wi, wo)

time: 93.8 us -> 94.7 us (level)
    pallas_call x1, Pallas kernels: 12.2 us -> 17.5 us  [attention(): pl.pallas_call(partial(attention_kernel, 4), out_shape=(jax.ShapeDtypeStr...]
    pallas_call x1, Pallas kernels: 45.4 us -> 41 us  [finish(): pl.pallas_call(finish_kernel, out_shape=tuple((jax.ShapeDtypeStruct(shape...]
where the time goes in v5:
time: 94.7 us; the launch traced here: 94.5 us
  Pallas kernels  93.9 us (99%)
    pallas_call x1, Pallas kernels, finish(): pl.pallas_call(finish_kernel, out_shape=tuple((jax.ShapeDtypeStruct(shape...  41 us
    pallas_call x1, Pallas kernels, project(): pl.pallas_call(project_kernel, out_shape=(jax.ShapeDtypeStruct(counts.sha...  31.5 us
    pallas_call x1, Pallas kernels, attention(): pl.pallas_call(partial(attention_kernel, 4), out_shape=(jax.ShapeDtypeStr...  17.5 us
    pallas_call x1, Pallas kernels, emit(): pl.pallas_call(partial(emit_kernel, factor), grid=(2,), out_shape=tuple((...  3.85 us

profile of v5, /device:TPU:1, one launch (start us, length us, event | category | flops | bytes accessed | tf_op | source)
XLA Modules:
  0.0 94.5 jit_solution(7592396431579183378)
XLA Ops:
  0.6 31.5 %project.1 = (s32[1,32]{1,0:T(1,128)}, bf16[4096,512]{1,0:T(8,128)(2,1)}, bf16[4096,128]{1,0:T(8,128)(2,1)}, bf16[128,4096]{1,0:T(8,128)(2,1)}, bf16[64,4096]{1,0:T(8,128)(2,1)}, /*index=5*/bf16[64,4096]{1,0:T(8,128)(2,1)}) custom-call(bf16[512,512]{1,0:T(8,128)(2,1)} %bitcast.12, bf16[512,512]{1,0:T(8,128)(2,1)} %bitcast.14, bf16[512,1536]{1,0:T(8,128)(2,1)} %wi_hbm.3, ...), custom_call_target="tpu_custom_call" | custom-call | tf_op jit(solution)/shard_map/project/pallas_call | solution.py:212
  32.2 17.5 %attention.1 = (bf16[256,4096]{1,0:T(8,128)(2,1)}, f32[192,512]{1,0:T(8,128)}) custom-call(s32[1,32]{1,0:T(1,128)} %get-tuple-element.20.order_ref, s32[8,32]{1,0:T(8,128)} %bitcast.17, s32[32]{0:T(128)} %bitcast.19, bf16[4096,128]{1,0:T(8,128)(2,1)} %get-tuple-element.21.kv_ref, bf16[128,4096]{1,0:T(8,128)(2,1)} %get-tuple-element.22.kvt_ref, ...), custom_call_target="tpu_custom_call" | custom-call | tf_op jit(solution)/shard_map/attention/pallas_call | solution.py:305
  49.7 41.0 %finish.1 = (bf16[512,512]{1,0:T(8,128)(2,1)}, bf16[512,512]{1,0:T(8,128)(2,1)}, bf16[512,512]{1,0:T(8,128)(2,1)}, bf16[512,1536]{1,0:T(8,128)(2,1)}) custom-call(bf16[4,64,4096]{2,1,0:T(8,128)(2,1)} %bitcast.11, f32[3,64,512]{2,1,0:T(8,128)} %bitcast.16, bf16[512,512]{1,0:T(8,128)(2,1)} %bitcast.13, bf16[512,512]{1,0:T(8,128)(2,1)} %bitcast.15, ...), custom_call_target="tpu_custom_call" | custom-call | tf_op jit(solution)/shard_map/finish/pallas_call | solution.py:577
  90.7 3.9 %emit.1 = (bf16[512,512]{1,0:T(8,128)(2,1)}, bf16[512,512]{1,0:T(8,128)(2,1)}, f32[512,512]{1,0:T(8,128)}, f32[512,1536]{1,0:T(8,128)}) custom-call(bf16[512,512]{1,0:T(8,128)(2,1)} %get-tuple-element.28.layer_ref, bf16[512,512]{1,0:T(8,128)(2,1)} %get-tuple-element.29.gradf_ref, bf16[512,512]{1,0:T(8,128)(2,1)} %get-tuple-element.30.osum_ref, ...), custom_call_target="tpu_custom_call" | custom-call | tf_op jit(solution)/shard_map/emit/pallas_call | solution.py:622

commit v6 on v5

--- a/solution.py
+++ b/solution.py
@@ -21,6 +21,7 @@
 TN = (((0,), (0,)), ((), ()))
 SIDE = 4
 VMEM_BYTES = 60 << 20
+CALM = 1600.0
 
 
 def dot(a, b, dims=NN):
@@ -73,7 +74,7 @@
 
 def project_kernel(
     x_hbm, g_hbm, wi_hbm, wo_hbm, count_ref,
-    order_ref, all_hbm, kv_hbm, kvt_hbm, qt_hbm, gt_hbm,
+    order_ref, reach_ref, all_hbm, kv_hbm, kvt_hbm, qt_hbm, gt_hbm,
     x_ref, kv_ref, kvt_ref, qt_ref, g_ref, wi_ref, wo_ref, grad_ref, send_sem, recv_sem, load_sem, store_sem,
 ):
     dp, seq = lax.axis_index("dp"), lax.axis_index("seq")
@@ -120,7 +121,7 @@
         chosen.append(jnp.where(core == 0, block[:, :HD], block[:, HD:]))
     chosen[2] = chosen[2] * jnp.asarray(SCALE, BF16)
     weights = jnp.concatenate(chosen + [jnp.zeros_like(chosen[0])], 1)
-    stores = []
+    stores, largest = [], [None, None]
 
     def store(source, target):
         stores.append(pltpu.make_async_copy(source, target, store_sem.at[len(stores)]))
@@ -130,9 +131,13 @@
         here = part(2 * source + h, half)
         product = dot(x_ref[source, rows(h), :], weights)
         kv = product[:, : 2 * HD].astype(BF16)
+        kvt, qt = kv.T, product[:, 2 * HD :].T[:HD].astype(BF16)
         kv_ref[here, :] = kv
-        kvt_ref[:, here] = kv.T
-        qt_ref[:, here] = product[:, 2 * HD :].T[:HD].astype(BF16)
+        kvt_ref[:, here] = kvt
+        qt_ref[:, here] = qt
+        for k, rows_of in enumerate((kvt[:HD], qt)):
+            norms = jnp.sum(jnp.square(rows_of.astype(F32)), 0, keepdims=True)
+            largest[k] = norms if largest[k] is None else jnp.maximum(largest[k], norms)
         store(x_ref.at[source, rows(h)], all_hbm.at[here, :])
         store(kv_ref.at[here, :], kv_hbm.at[here, :])
         store(kvt_ref.at[:, here], kvt_hbm.at[:, here])
@@ -193,6 +198,8 @@
     project_arrived(5)
     arrive_near(12, at(2, 1), 0)
     arrive_near(13, at(2, 1), 1)
+    reach = jnp.max(largest[0], 1, keepdims=True) * jnp.max(largest[1], 1, keepdims=True)
+    reach_ref[...] = jnp.broadcast_to(reach, reach_ref.shape)
     for copy in sent:
         copy.wait_send()
     for copy in stores:
@@ -213,6 +220,7 @@
         project_kernel,
         out_shape=(
             jax.ShapeDtypeStruct(counts.shape, jnp.int32),
+            jax.ShapeDtypeStruct((1, B), F32),
             jax.ShapeDtypeStruct((span, width), BF16),
             jax.ShapeDtypeStruct((span, 2 * HD), BF16),
             jax.ShapeDtypeStruct((2 * HD, span), BF16),
@@ -220,7 +228,7 @@
             jax.ShapeDtypeStruct((HD, span), BF16),
         ),
         in_specs=[anywhere] * 4 + [vm],
-        out_specs=(vm,) + (anywhere,) * 5,
+        out_specs=(vm, vm) + (anywhere,) * 5,
         scratch_shapes=[
             pltpu.VMEM((H, nodes, width), BF16),
             pltpu.VMEM((span, 2 * HD), BF16),
@@ -241,7 +249,7 @@
 
 
 def attention_kernel(
-    group, order_ref, blocks_ref, counts_ref, kv_ref, kvt_ref, qt_ref, gt_ref, all_hbm, grads_ref, weight_ref,
+    group, order_ref, reach_ref, blocks_ref, counts_ref, kv_ref, kvt_ref, qt_ref, gt_ref, all_hbm, grads_ref, weight_ref,
     total_ref, all_ref, load_sem,
 ):
     block_count = kvt_ref.shape[1] // B
@@ -250,7 +258,7 @@
     total_ref[...] = jnp.zeros_like(total_ref)
     zero = jnp.zeros((HD, B), BF16)
 
-    def query_blocks(ids, live):
+    def query_blocks(ids, live, shifted):
         heres = [pl.ds(pl.multiple_of(i * B, B), B) for i in ids]
         spots = [[pl.ds(pl.multiple_of(blocks_ref[j, i] * B, B), B) for j in range(live)] for i in ids]
         aparts, products = [], []
@@ -268,7 +276,9 @@
                 scores.append(product[j * B : (j + 1) * B, :B] + jnp.where(j < count, 0.0, NEGATIVE))
             scores = jnp.concatenate(scores, 0)
             grad_probs = product[:, B:]
-            raised = jnp.exp(scores - jnp.max(scores, 0, keepdims=True))
+            if shifted:
+                scores = scores - jnp.max(scores, 0, keepdims=True)
+            raised = jnp.exp(scores)
             inverse = 1.0 / jnp.sum(raised, 0, keepdims=True)
             row_delta = jnp.sum(raised * grad_probs, 0, keepdims=True) * inverse
             probs = raised * inverse
@@ -289,23 +299,36 @@
         ids = [order_ref[0, index * group + t] for t in range(group)]
         most = counts_ref[ids[0]]
         for live in range(1, KMAX + 1):
-            pl.when(most == live)(partial(query_blocks, ids, live))
+            pl.when(most == live)(partial(query_blocks, ids, live, False))
         return carry
 
-    lax.fori_loop(0, block_count // group, step, 0)
+    def step_shifted(index, carry):
+        query_blocks([index], KMAX, True)
+        return carry
+
+    calm = reach_ref[0, 0] <= CALM
+
+    @pl.when(calm)
+    def _():
+        lax.fori_loop(0, block_count // group, step, 0)
+
+    @pl.when(jnp.logical_not(calm))
+    def _():
+        lax.fori_loop(0, block_count, step_shifted, 0)
+
     grads_ref[2 * HD :, :] = total_ref[...].astype(BF16)
     load.wait()
     weight_ref[...] = dot(grads_ref[HD:, :], all_ref[...])
 
 
-def attention(order, blocks, counts, kv, kvt, qt, gt, everything):
+def attention(order, reach, blocks, counts, kv, kvt, qt, gt, everything):
     span, width = everything.shape
     vm = pl.BlockSpec(memory_space=pltpu.VMEM)
     sm = pl.BlockSpec(memory_space=pltpu.SMEM)
     return pl.pallas_call(
         partial(attention_kernel, 4),
         out_shape=(jax.ShapeDtypeStruct((4 * HD, span), BF16), jax.ShapeDtypeStruct((3 * HD, width), F32)),
-        in_specs=[sm, sm, sm, vm, vm, vm, vm, pl.BlockSpec(memory_space=pl.ANY)],
+        in_specs=[sm, sm, sm, sm, vm, vm, vm, vm, pl.BlockSpec(memory_space=pl.ANY)],
         out_specs=(vm, vm),
         scratch_shapes=[
             pltpu.VMEM((2 * HD, span), F32),
@@ -314,7 +337,7 @@
         ],
         compiler_params=pltpu.CompilerParams(vmem_limit_bytes=VMEM_BYTES),
         name="attention",
-    )(order, blocks, counts, kv, kvt, qt, gt, everything)
+    )(order, reach, blocks, counts, kv, kvt, qt, gt, everything)
 
 
 ROWS = (256, 64, 16)
@@ -510,19 +533,19 @@
     right.scatter_first(merged[:, half:])
     back_k += back_rows(1, 1)
 
-    layer_ref[...] = (x_ref[...].astype(F32) + dot(attended_ref[...], wo_ref[...], TN)).astype(BF16)
-    store(layer_ref, layer_hbm)
+    left.scatter_second()
+    right.scatter_second()
     for copy in spread:
         copy.wait_recv()
     both.gather()
     last.gather()
-    left.scatter_second()
-    right.scatter_second()
-    both.gather_on()
-    last.gather_on()
     left.exchange("y", y)
     right.exchange("y", y)
     back_v = back_rows(2, 0) + back_rows(2, 1)
+    both.gather_on()
+    last.gather_on()
+    layer_ref[...] = (x_ref[...].astype(F32) + dot(attended_ref[...], wo_ref[...], TN)).astype(BF16)
+    store(layer_ref, layer_hbm)
     for copy in back_q:
         copy.wait_recv()
     total_ref[...] = dot(wi_ref[:, :width], rows_ref[0])
@@ -632,8 +655,8 @@
 
 def shards(features, input_weight, output_weight, key_blocks, key_count, cotangent):
     x, g = features[0], cotangent[0]
-    order, everything, kv, kvt, qt, gt = project(x, g, input_weight, output_weight, key_count[0])
-    grads, weight = attention(order, key_blocks[0, 0].T, key_count[0, 0], kv, kvt, qt, gt, everything)
+    order, reach, everything, kv, kvt, qt, gt = project(x, g, input_weight, output_weight, key_count[0])
+    grads, weight = attention(order, reach, key_blocks[0, 0].T, key_count[0, 0], kv, kvt, qt, gt, everything)
     results = finish(grads, weight, x, g, input_weight, output_weight)
     factor = 1.0 / (lax.axis_size("dp") * lax.axis_size("seq") * x.shape[0]) ** 0.5
     layer_out, grad_features, output_total, input_total = emit(*results, factor)

time: 94.7 us -> 118 us (1.25)
  Pallas kernels: 93.9 us -> 118 us
    pallas_call x1, Pallas kernels: 17.5 us -> 41.7 us  [attention(): pl.pallas_call(partial(attention_kernel, 4), out_shape=(jax.ShapeDtypeStr...]
where the time goes in v6:
time: 118 us
  Pallas kernels  118 us (100%)
    pallas_call x1, Pallas kernels, attention(): pl.pallas_call(partial(attention_kernel, 4), out_shape=(jax.ShapeDtypeStr...  41.7 us
    pallas_call x1, Pallas kernels, finish(): pl.pallas_call(finish_kernel, out_shape=tuple((jax.ShapeDtypeStruct(shape...  40.5 us
    pallas_call x1, Pallas kernels, project(): pl.pallas_call(project_kernel, out_shape=(jax.ShapeDtypeStruct(counts.sha...  31.5 us
    pallas_call x1, Pallas kernels, emit(): pl.pallas_call(partial(emit_kernel, factor), grid=(2,), out_shape=tuple((...  3.85 us

profile of v6, /device:TPU:1, one launch (start us, length us, event | category | flops | bytes accessed | tf_op | source)
XLA Modules:
  0.0 118.2 jit_solution(10109619530813493042)
XLA Ops:
  0.6 31.5 %project.1 = (s32[1,32]{1,0:T(1,128)}, f32[1,128]{1,0:T(1,128)}, bf16[4096,512]{1,0:T(8,128)(2,1)}, bf16[4096,128]{1,0:T(8,128)(2,1)}, bf16[128,4096]{1,0:T(8,12...) custom-call(bf16[512,512]{1,0:T(8,128)(2,1)} %bitcast.12, bf16[512,512]{1,0:T(8,128)(2,1)} %bitcast.14, ...), custom_call_target="tpu_custom_call" | custom-call | tf_op jit(solution)/shard_map/project/pallas_call | solution.py:219
  32.2 41.7 %attention.1 = (bf16[256,4096]{1,0:T(8,128)(2,1)}, f32[192,512]{1,0:T(8,128)}) custom-call(s32[1,32]{1,0:T(1,128)} %get-tuple-element.21.order_ref, f32[1,128]{1,0:T(1,128)} %get-tuple-element.22.reach_ref, s32[8,32]{1,0:T(8,128)} %bitcast.17, s32[32]{0:T(128)} %bitcast.19, bf16[4096,128]{1,0:T(8,128)(2,1)} %get-tuple-element.23.kv_ref, ...), custom_call_target="tpu_custom_call" | custom-call | tf_op jit(solution)/shard_map/attention/pallas_call | solution.py:328
  73.9 40.5 %finish.1 = (bf16[512,512]{1,0:T(8,128)(2,1)}, bf16[512,512]{1,0:T(8,128)(2,1)}, bf16[512,512]{1,0:T(8,128)(2,1)}, bf16[512,1536]{1,0:T(8,128)(2,1)}) custom-call(bf16[4,64,4096]{2,1,0:T(8,128)(2,1)} %bitcast.11, f32[3,64,512]{2,1,0:T(8,128)} %bitcast.16, bf16[512,512]{1,0:T(8,128)(2,1)} %bitcast.13, bf16[512,512]{1,0:T(8,128)(2,1)} %bitcast.15, ...), custom_call_target="tpu_custom_call" | custom-call | tf_op jit(solution)/shard_map/finish/pallas_call | solution.py:600
  114.4 3.9 %emit.1 = (bf16[512,512]{1,0:T(8,128)(2,1)}, bf16[512,512]{1,0:T(8,128)(2,1)}, f32[512,512]{1,0:T(8,128)}, f32[512,1536]{1,0:T(8,128)}) custom-call(bf16[512,512]{1,0:T(8,128)(2,1)} %get-tuple-element.30.layer_ref, bf16[512,512]{1,0:T(8,128)(2,1)} %get-tuple-element.31.gradf_ref, bf16[512,512]{1,0:T(8,128)(2,1)} %get-tuple-element.32.osum_ref, ...), custom_call_target="tpu_custom_call" | custom-call | tf_op jit(solution)/shard_map/emit/pallas_call | solution.py:645

commit v7 on v6

--- a/solution.py
+++ b/solution.py
@@ -249,13 +249,21 @@
 
 
 def attention_kernel(
-    group, order_ref, reach_ref, blocks_ref, counts_ref, kv_ref, kvt_ref, qt_ref, gt_ref, all_hbm, grads_ref, weight_ref,
-    total_ref, all_ref, load_sem,
+    group, order_ref, reach_ref, blocks_ref, counts_ref, kv_hbm, kvt_hbm, qt_hbm, gt_hbm, all_hbm, grads_hbm, weight_hbm,
+    kv_ref, kvt_ref, qt_ref, gt_ref, all_ref, grads_ref, weight_ref, total_ref, load_sem, store_sem,
 ):
     block_count = kvt_ref.shape[1] // B
-    load = pltpu.make_async_copy(all_hbm, all_ref, load_sem)
-    load.start()
+    loads = [
+        pltpu.make_async_copy(source, target, load_sem.at[k])
+        for k, (source, target) in enumerate(
+            ((kv_hbm, kv_ref), (qt_hbm, qt_ref), (gt_hbm, gt_ref), (kvt_hbm, kvt_ref), (all_hbm, all_ref))
+        )
+    ]
+    for load in loads:
+        load.start()
     total_ref[...] = jnp.zeros_like(total_ref)
+    for load in loads[:4]:
+        load.wait()
     zero = jnp.zeros((HD, B), BF16)
 
     def query_blocks(ids, live, shifted):
@@ -316,28 +324,45 @@
     def _():
         lax.fori_loop(0, block_count, step_shifted, 0)
 
+    stores = [
+        pltpu.make_async_copy(source, target, store_sem.at[k])
+        for k, (source, target) in enumerate(
+            (
+                (grads_ref.at[pl.ds(0, 2 * HD), :], grads_hbm.at[pl.ds(0, 2 * HD), :]),
+                (grads_ref.at[pl.ds(2 * HD, 2 * HD), :], grads_hbm.at[pl.ds(2 * HD, 2 * HD), :]),
+                (weight_ref, weight_hbm),
+            )
+        )
+    ]
+    stores[0].start()
     grads_ref[2 * HD :, :] = total_ref[...].astype(BF16)
-    load.wait()
+    stores[1].start()
+    loads[4].wait()
     weight_ref[...] = dot(grads_ref[HD:, :], all_ref[...])
-
-
-def attention(order, reach, blocks, counts, kv, kvt, qt, gt, everything):
-    span, width = everything.shape
-    vm = pl.BlockSpec(memory_space=pltpu.VMEM)
+    stores[2].start()
+    for store in stores:
+        store.wait()
+
+
+def attention(order, reach, blocks, counts, *arrays):
+    span, width = arrays[-1].shape
     sm = pl.BlockSpec(memory_space=pltpu.SMEM)
+    anywhere = pl.BlockSpec(memory_space=pl.ANY)
+    results = (jax.ShapeDtypeStruct((4 * HD, span), BF16), jax.ShapeDtypeStruct((3 * HD, width), F32))
     return pl.pallas_call(
         partial(attention_kernel, 4),
-        out_shape=(jax.ShapeDtypeStruct((4 * HD, span), BF16), jax.ShapeDtypeStruct((3 * HD, width), F32)),
-        in_specs=[sm, sm, sm, sm, vm, vm, vm, vm, pl.BlockSpec(memory_space=pl.ANY)],
-        out_specs=(vm, vm),
-        scratch_shapes=[
+        out_shape=results,
+        in_specs=[sm] * 4 + [anywhere] * len(arrays),
+        out_specs=(anywhere,) * 2,
+        scratch_shapes=[pltpu.VMEM(a.shape, a.dtype) for a in arrays + results]
+        + [
             pltpu.VMEM((2 * HD, span), F32),
-            pltpu.VMEM(everything.shape, BF16),
-            pltpu.SemaphoreType.DMA,
+            pltpu.SemaphoreType.DMA((len(arrays),)),
+            pltpu.SemaphoreType.DMA((3,)),
         ],
         compiler_params=pltpu.CompilerParams(vmem_limit_bytes=VMEM_BYTES),
         name="attention",
-    )(order, reach, blocks, counts, kv, kvt, qt, gt, everything)
+    )(order, reach, blocks, counts, *arrays)
 
 
 ROWS = (256, 64, 16)
@@ -500,7 +525,7 @@
     merged_ref[:, part(1 - core, HD), :] = theirs_ref[...]
     both.scatter_first(jnp.concatenate([merged_ref[0].T, merged_ref[1].T], 1))
     last.scatter_first(merged_ref[2].T)
-    back_q = back_rows(0, 0)
+    back_q = back_rows(0, 0) + back_rows(0, 1)
     for load in loads[1:]:
         load.wait()
     both.scatter_second()
@@ -508,11 +533,16 @@
 
     for copy in back_attended:
         copy.wait_recv()
-    total_ref[...] = dot(attended_ref[...], g_ref[...])
-    half_ref[0] = total_ref[part(1 - core, ROWS[0]), :].astype(BF16)
+    half_ref[0] = dot(attended_ref[part(1 - core, ROWS[0]), :], g_ref[...]).astype(BF16)
     merge = remote(half_ref.at[0], half_ref.at[1], core_sems, 1, other)
     merge.start()
     sent.append(merge)
+    total_ref[0 : ROWS[0], :] = dot(attended_ref[part(core, ROWS[0]), :], g_ref[...])
+
+    merge.wait_recv()
+    merged = total_ref[0 : ROWS[0], :] + half_ref[1].astype(F32)
+    left.scatter_first(merged[:, :half])
+    right.scatter_first(merged[:, half:])
 
     spread = []
     for job, kinds in ((both, (0, 1)), (last, (2,))):
@@ -525,14 +555,7 @@
                 spread.append(remote(here, here, (spread_send, spread_recv), (kind, offset - 1), along("y", offset)))
                 spread[-1].start()
     sent.extend(spread)
-    back_q += back_rows(0, 1)
-    back_k = back_rows(1, 0)
-    merge.wait_recv()
-    merged = total_ref[part(core, ROWS[0]), :] + half_ref[1].astype(F32)
-    left.scatter_first(merged[:, :half])
-    right.scatter_first(merged[:, half:])
-    back_k += back_rows(1, 1)
-
+    back_k = back_rows(1, 0) + back_rows(1, 1)
     left.scatter_second()
     right.scatter_second()
     for copy in spread:

time: 118 us -> 118 us (level)
  no operation moved by 1% of the time
where the time goes in v7:
time: 118 us
  Pallas kernels  117 us (99%)
    pallas_call x1, Pallas kernels, attention(): pl.pallas_call(partial(attention_kernel, 4), out_shape=results, in_specs=...  42.2 us
    pallas_call x1, Pallas kernels, finish(): pl.pallas_call(finish_kernel, out_shape=tuple((jax.ShapeDtypeStruct(shape...  39.4 us
    pallas_call x1, Pallas kernels, project(): pl.pallas_call(project_kernel, out_shape=(jax.ShapeDtypeStruct(counts.sha...  31.5 us
    pallas_call x1, Pallas kernels, emit(): pl.pallas_call(partial(emit_kernel, factor), grid=(2,), out_shape=tuple((...  3.85 us

profile of v7, /device:TPU:1, one launch (start us, length us, event | category | flops | bytes accessed | tf_op | source)
XLA Modules:
  0.0 117.6 jit_solution(8368467832449527812)
XLA Ops:
  0.6 31.5 %project.1 = (s32[1,32]{1,0:T(1,128)}, f32[1,128]{1,0:T(1,128)}, bf16[4096,512]{1,0:T(8,128)(2,1)}, bf16[4096,128]{1,0:T(8,128)(2,1)}, bf16[128,4096]{1,0:T(8,12...) custom-call(bf16[512,512]{1,0:T(8,128)(2,1)} %bitcast.12, bf16[512,512]{1,0:T(8,128)(2,1)} %bitcast.14, ...), custom_call_target="tpu_custom_call" | custom-call | tf_op jit(solution)/shard_map/project/pallas_call | solution.py:219
  32.2 42.2 %attention.1 = (bf16[256,4096]{1,0:T(8,128)(2,1)}, f32[192,512]{1,0:T(8,128)}) custom-call(s32[1,32]{1,0:T(1,128)} %get-tuple-element.21.order_ref, f32[1,128]{1,0:T(1,128)} %get-tuple-element.22.reach_ref, s32[8,32]{1,0:T(8,128)} %bitcast.17, s32[32]{0:T(128)} %bitcast.19, bf16[4096,128]{1,0:T(8,128)(2,1)} %get-tuple-element.23.kv_hbm, ...), custom_call_target="tpu_custom_call" | custom-call | tf_op jit(solution)/shard_map/attention/pallas_call | solution.py:352
  74.4 39.4 %finish.1 = (bf16[512,512]{1,0:T(8,128)(2,1)}, bf16[512,512]{1,0:T(8,128)(2,1)}, bf16[512,512]{1,0:T(8,128)(2,1)}, bf16[512,1536]{1,0:T(8,128)(2,1)}) custom-call(bf16[4,64,4096]{2,1,0:T(8,128)(2,1)} %bitcast.11, f32[3,64,512]{2,1,0:T(8,128)} %bitcast.16, bf16[512,512]{1,0:T(8,128)(2,1)} %bitcast.13, bf16[512,512]{1,0:T(8,128)(2,1)} %bitcast.15, ...), custom_call_target="tpu_custom_call" | custom-call | tf_op jit(solution)/shard_map/finish/pallas_call | solution.py:623
  113.8 3.9 %emit.1 = (bf16[512,512]{1,0:T(8,128)(2,1)}, bf16[512,512]{1,0:T(8,128)(2,1)}, f32[512,512]{1,0:T(8,128)}, f32[512,1536]{1,0:T(8,128)}) custom-call(bf16[512,512]{1,0:T(8,128)(2,1)} %get-tuple-element.30.layer_ref, bf16[512,512]{1,0:T(8,128)(2,1)} %get-tuple-element.31.gradf_ref, bf16[512,512]{1,0:T(8,128)(2,1)} %get-tuple-element.32.osum_ref, ...), custom_call_target="tpu_custom_call" | custom-call | tf_op jit(solution)/shard_map/emit/pallas_call | solution.py:668

commit v8 on v7

--- a/solution.py
+++ b/solution.py
@@ -46,7 +46,7 @@
     barrier = pltpu.get_barrier_semaphore()
     for device in devices:
         pl.semaphore_signal(barrier, inc=1, device_id=device, device_id_type=MESH)
-    pl.semaphore_wait(barrier, len(devices))
+    return partial(pl.semaphore_wait, barrier, len(devices))
 
 
 def remote(source, target, sems, index, device):
@@ -88,6 +88,7 @@
         return ((y + dy) % SIDE) * 2 + (core + flip) % 2
 
     peers = seq_peers(seq)
+    met = greet([(dp, peer) for peer in peers])
     loads = [
         pltpu.make_async_copy(source, target, load_sem.at[k])
         for k, (source, target) in enumerate(
@@ -96,7 +97,7 @@
     ]
     for load in loads:
         load.start()
-    greet([(dp, peer) for peer in peers])
+    met()
     up, down = (dp, at(1)), (dp, at(3))
 
     def rows(h):
@@ -259,11 +260,12 @@
             ((kv_hbm, kv_ref), (qt_hbm, qt_ref), (gt_hbm, gt_ref), (kvt_hbm, kvt_ref), (all_hbm, all_ref))
         )
     ]
-    for load in loads:
+    for load in loads[:4]:
         load.start()
     total_ref[...] = jnp.zeros_like(total_ref)
     for load in loads[:4]:
         load.wait()
+    loads[4].start()
     zero = jnp.zeros((HD, B), BF16)
 
     def query_blocks(ids, live, shifted):
@@ -467,6 +469,8 @@
             return (z * SIDE + (x + offset) % SIDE, seq)
         return (((z + offset) % SIDE) * SIDE + x, seq)
 
+    peers = seq_peers(seq)
+    met = greet([(dp, peer) for peer in peers] + [along(axis, offset) for axis in ("x", "z") for offset in (1, 2, 3)])
     loads = [
         pltpu.make_async_copy(source, target, load_sem.at[k])
         for k, (source, target) in enumerate(
@@ -483,8 +487,7 @@
     ]
     for load in loads:
         load.start()
-    peers = seq_peers(seq)
-    greet([(dp, peer) for peer in peers] + [along(axis, offset) for axis in ("x", "z") for offset in (1, 2, 3)])
+    met()
 
     sent, stores = [], []
 

time: 118 us -> 118 us (level)
  no operation moved by 1% of the time
where the time goes in v8:
time: 118 us
  Pallas kernels  117 us (99%)
    pallas_call x1, Pallas kernels, attention(): pl.pallas_call(partial(attention_kernel, 4), out_shape=results, in_specs=...  42.2 us
    pallas_call x1, Pallas kernels, finish(): pl.pallas_call(finish_kernel, out_shape=tuple((jax.ShapeDtypeStruct(shape...  39.5 us
    pallas_call x1, Pallas kernels, project(): pl.pallas_call(project_kernel, out_shape=(jax.ShapeDtypeStruct(counts.sha...  31.5 us
    pallas_call x1, Pallas kernels, emit(): pl.pallas_call(partial(emit_kernel, factor), grid=(2,), out_shape=tuple((...  3.85 us

profile of v8, /device:TPU:1, one launch (start us, length us, event | category | flops | bytes accessed | tf_op | source)
XLA Modules:
  0.0 117.7 jit_solution(15797379307727701799)
XLA Ops:
  0.6 31.5 %project.1 = (s32[1,32]{1,0:T(1,128)}, f32[1,128]{1,0:T(1,128)}, bf16[4096,512]{1,0:T(8,128)(2,1)}, bf16[4096,128]{1,0:T(8,128)(2,1)}, bf16[128,4096]{1,0:T(8,12...) custom-call(bf16[512,512]{1,0:T(8,128)(2,1)} %bitcast.12, bf16[512,512]{1,0:T(8,128)(2,1)} %bitcast.14, ...), custom_call_target="tpu_custom_call" | custom-call | tf_op jit(solution)/shard_map/project/pallas_call | solution.py:220
  32.2 42.2 %attention.1 = (bf16[256,4096]{1,0:T(8,128)(2,1)}, f32[192,512]{1,0:T(8,128)}) custom-call(s32[1,32]{1,0:T(1,128)} %get-tuple-element.21.order_ref, f32[1,128]{1,0:T(1,128)} %get-tuple-element.22.reach_ref, s32[8,32]{1,0:T(8,128)} %bitcast.17, s32[32]{0:T(128)} %bitcast.19, bf16[4096,128]{1,0:T(8,128)(2,1)} %get-tuple-element.23.kv_hbm, ...), custom_call_target="tpu_custom_call" | custom-call | tf_op jit(solution)/shard_map/attention/pallas_call | solution.py:354
  74.4 39.5 %finish.1 = (bf16[512,512]{1,0:T(8,128)(2,1)}, bf16[512,512]{1,0:T(8,128)(2,1)}, bf16[512,512]{1,0:T(8,128)(2,1)}, bf16[512,1536]{1,0:T(8,128)(2,1)}) custom-call(bf16[4,64,4096]{2,1,0:T(8,128)(2,1)} %bitcast.11, f32[3,64,512]{2,1,0:T(8,128)} %bitcast.16, bf16[512,512]{1,0:T(8,128)(2,1)} %bitcast.13, bf16[512,512]{1,0:T(8,128)(2,1)} %bitcast.15, ...), custom_call_target="tpu_custom_call" | custom-call | tf_op jit(solution)/shard_map/finish/pallas_call | solution.py:626
  113.9 3.9 %emit.1 = (bf16[512,512]{1,0:T(8,128)(2,1)}, bf16[512,512]{1,0:T(8,128)(2,1)}, f32[512,512]{1,0:T(8,128)}, f32[512,1536]{1,0:T(8,128)}) custom-call(bf16[512,512]{1,0:T(8,128)(2,1)} %get-tuple-element.30.layer_ref, bf16[512,512]{1,0:T(8,128)(2,1)} %get-tuple-element.31.gradf_ref, bf16[512,512]{1,0:T(8,128)(2,1)} %get-tuple-element.32.osum_ref, ...), custom_call_target="tpu_custom_call" | custom-call | tf_op jit(solution)/shard_map/emit/pallas_call | solution.py:671

commit v9 on v6

--- a/solution.py
+++ b/solution.py
@@ -46,7 +46,7 @@
     barrier = pltpu.get_barrier_semaphore()
     for device in devices:
         pl.semaphore_signal(barrier, inc=1, device_id=device, device_id_type=MESH)
-    pl.semaphore_wait(barrier, len(devices))
+    return partial(pl.semaphore_wait, barrier, len(devices))
 
 
 def remote(source, target, sems, index, device):
@@ -88,6 +88,7 @@
         return ((y + dy) % SIDE) * 2 + (core + flip) % 2
 
     peers = seq_peers(seq)
+    met = greet([(dp, peer) for peer in peers])
     loads = [
         pltpu.make_async_copy(source, target, load_sem.at[k])
         for k, (source, target) in enumerate(
@@ -96,7 +97,7 @@
     ]
     for load in loads:
         load.start()
-    greet([(dp, peer) for peer in peers])
+    met()
     up, down = (dp, at(1)), (dp, at(3))
 
     def rows(h):
@@ -442,6 +443,8 @@
             return (z * SIDE + (x + offset) % SIDE, seq)
         return (((z + offset) % SIDE) * SIDE + x, seq)
 
+    peers = seq_peers(seq)
+    met = greet([(dp, peer) for peer in peers] + [along(axis, offset) for axis in ("x", "z") for offset in (1, 2, 3)])
     loads = [
         pltpu.make_async_copy(source, target, load_sem.at[k])
         for k, (source, target) in enumerate(
@@ -458,8 +461,7 @@
     ]
     for load in loads:
         load.start()
-    peers = seq_peers(seq)
-    greet([(dp, peer) for peer in peers] + [along(axis, offset) for axis in ("x", "z") for offset in (1, 2, 3)])
+    met()
 
     sent, stores = [], []
 
@@ -500,7 +502,7 @@
     merged_ref[:, part(1 - core, HD), :] = theirs_ref[...]
     both.scatter_first(jnp.concatenate([merged_ref[0].T, merged_ref[1].T], 1))
     last.scatter_first(merged_ref[2].T)
-    back_q = back_rows(0, 0)
+    back_q = back_rows(0, 0) + back_rows(0, 1)
     for load in loads[1:]:
         load.wait()
     both.scatter_second()
@@ -508,11 +510,16 @@
 
     for copy in back_attended:
         copy.wait_recv()
-    total_ref[...] = dot(attended_ref[...], g_ref[...])
-    half_ref[0] = total_ref[part(1 - core, ROWS[0]), :].astype(BF16)
+    half_ref[0] = dot(attended_ref[part(1 - core, ROWS[0]), :], g_ref[...]).astype(BF16)
     merge = remote(half_ref.at[0], half_ref.at[1], core_sems, 1, other)
     merge.start()
     sent.append(merge)
+    total_ref[0 : ROWS[0], :] = dot(attended_ref[part(core, ROWS[0]), :], g_ref[...])
+
+    merge.wait_recv()
+    merged = total_ref[0 : ROWS[0], :] + half_ref[1].astype(F32)
+    left.scatter_first(merged[:, :half])
+    right.scatter_first(merged[:, half:])
 
     spread = []
     for job, kinds in ((both, (0, 1)), (last, (2,))):
@@ -525,14 +532,7 @@
                 spread.append(remote(here, here, (spread_send, spread_recv), (kind, offset - 1), along("y", offset)))
                 spread[-1].start()
     sent.extend(spread)
-    back_q += back_rows(0, 1)
-    back_k = back_rows(1, 0)
-    merge.wait_recv()
-    merged = total_ref[part(core, ROWS[0]), :] + half_ref[1].astype(F32)
-    left.scatter_first(merged[:, :half])
-    right.scatter_first(merged[:, half:])
-    back_k += back_rows(1, 1)
-
+    back_k = back_rows(1, 0) + back_rows(1, 1)
     left.scatter_second()
     right.scatter_second()
     for copy in spread:

time: 118 us -> 117 us (level)
  Pallas kernels: 118 us -> 116 us
where the time goes in v9:
time: 117 us
  Pallas kernels  116 us (99%)
    pallas_call x1, Pallas kernels, attention(): pl.pallas_call(partial(attention_kernel, 4), out_shape=(jax.ShapeDtypeStr...  41.7 us
    pallas_call x1, Pallas kernels, finish(): pl.pallas_call(finish_kernel, out_shape=tuple((jax.ShapeDtypeStruct(shape...  39.4 us
    pallas_call x1, Pallas kernels, project(): pl.pallas_call(project_kernel, out_shape=(jax.ShapeDtypeStruct(counts.sha...  31.5 us
    pallas_call x1, Pallas kernels, emit(): pl.pallas_call(partial(emit_kernel, factor), grid=(2,), out_shape=tuple((...  3.85 us

profile of v9, /device:TPU:1, one launch (start us, length us, event | category | flops | bytes accessed | tf_op | source)
XLA Modules:
  0.0 117.1 jit_solution(779316318201759099)
XLA Ops:
  0.6 31.5 %project.1 = (s32[1,32]{1,0:T(1,128)}, f32[1,128]{1,0:T(1,128)}, bf16[4096,512]{1,0:T(8,128)(2,1)}, bf16[4096,128]{1,0:T(8,128)(2,1)}, bf16[128,4096]{1,0:T(8,12...) custom-call(bf16[512,512]{1,0:T(8,128)(2,1)} %bitcast.12, bf16[512,512]{1,0:T(8,128)(2,1)} %bitcast.14, ...), custom_call_target="tpu_custom_call" | custom-call | tf_op jit(solution)/shard_map/project/pallas_call | solution.py:220
  32.2 41.7 %attention.1 = (bf16[256,4096]{1,0:T(8,128)(2,1)}, f32[192,512]{1,0:T(8,128)}) custom-call(s32[1,32]{1,0:T(1,128)} %get-tuple-element.21.order_ref, f32[1,128]{1,0:T(1,128)} %get-tuple-element.22.reach_ref, s32[8,32]{1,0:T(8,128)} %bitcast.17, s32[32]{0:T(128)} %bitcast.19, bf16[4096,128]{1,0:T(8,128)(2,1)} %get-tuple-element.23.kv_ref, ...), custom_call_target="tpu_custom_call" | custom-call | tf_op jit(solution)/shard_map/attention/pallas_call | solution.py:329
  73.9 39.4 %finish.1 = (bf16[512,512]{1,0:T(8,128)(2,1)}, bf16[512,512]{1,0:T(8,128)(2,1)}, bf16[512,512]{1,0:T(8,128)(2,1)}, bf16[512,1536]{1,0:T(8,128)(2,1)}) custom-call(bf16[4,64,4096]{2,1,0:T(8,128)(2,1)} %bitcast.11, f32[3,64,512]{2,1,0:T(8,128)} %bitcast.16, bf16[512,512]{1,0:T(8,128)(2,1)} %bitcast.13, bf16[512,512]{1,0:T(8,128)(2,1)} %bitcast.15, ...), custom_call_target="tpu_custom_call" | custom-call | tf_op jit(solution)/shard_map/finish/pallas_call | solution.py:600
  113.3 3.9 %emit.1 = (bf16[512,512]{1,0:T(8,128)(2,1)}, bf16[512,512]{1,0:T(8,128)(2,1)}, f32[512,512]{1,0:T(8,128)}, f32[512,1536]{1,0:T(8,128)}) custom-call(bf16[512,512]{1,0:T(8,128)(2,1)} %get-tuple-element.30.layer_ref, bf16[512,512]{1,0:T(8,128)(2,1)} %get-tuple-element.31.gradf_ref, bf16[512,512]{1,0:T(8,128)(2,1)} %get-tuple-element.32.osum_ref, ...), custom_call_target="tpu_custom_call" | custom-call | tf_op jit(solution)/shard_map/emit/pallas_call | solution.py:645

commit v10 on v9

--- a/solution.py
+++ b/solution.py
@@ -477,12 +477,9 @@
         sent.extend(copies)
         return copies
 
-    def back_rows(kind, h):
-        mine = pl.ds(h * half, half)
+    def back_rows(kind):
         return back(
-            1 + 2 * kind + h,
-            lambda peer: grads_hbm.at[1 + kind, :, part(2 * peer + h, half)],
-            rows_ref.at[kind, part(seq, HD), mine],
+            1 + kind, lambda peer: grads_hbm.at[1 + kind, :, part(peer, nodes)], rows_ref.at[kind, part(seq, HD), :]
         )
 
     swap = remote(weight_hbm.at[:, :, part(1 - core, ROWS[0])], theirs_ref, core_sems, 0, other)
@@ -502,7 +499,7 @@
     merged_ref[:, part(1 - core, HD), :] = theirs_ref[...]
     both.scatter_first(jnp.concatenate([merged_ref[0].T, merged_ref[1].T], 1))
     last.scatter_first(merged_ref[2].T)
-    back_q = back_rows(0, 0) + back_rows(0, 1)
+    back_q = back_rows(0)
     for load in loads[1:]:
         load.wait()
     both.scatter_second()
@@ -532,7 +529,7 @@
                 spread.append(remote(here, here, (spread_send, spread_recv), (kind, offset - 1), along("y", offset)))
                 spread[-1].start()
     sent.extend(spread)
-    back_k = back_rows(1, 0) + back_rows(1, 1)
+    back_k = back_rows(1)
     left.scatter_second()
     right.scatter_second()
     for copy in spread:
@@ -541,7 +538,7 @@
     last.gather()
     left.exchange("y", y)
     right.exchange("y", y)
-    back_v = back_rows(2, 0) + back_rows(2, 1)
+    back_v = back_rows(2)
     both.gather_on()
     last.gather_on()
     layer_ref[...] = (x_ref[...].astype(F32) + dot(attended_ref[...], wo_ref[...], TN)).astype(BF16)
@@ -620,7 +617,7 @@
         + [pltpu.VMEM((SIDE - 1, ROWS[1], n), BF16) for n in columns]
         + [pltpu.VMEM((SIDE - 1, ROWS[2], n), BF16) for n in columns]
         + [pltpu.VMEM((SIDE, ROWS[2], n), BF16) for n in columns[2:]]
-        + [dma((7, H - 1))] * 2
+        + [dma((4, H - 1))] * 2
         + [dma((4,))] * 2
         + [dma((4, 8, SIDE - 1))] * 2
         + [dma((3, SIDE - 1))] * 2

time: 117 us -> 118 us (level)
  no operation moved by 1% of the time
where the time goes in v10:
time: 118 us
  Pallas kernels  117 us (99%)
    pallas_call x1, Pallas kernels, attention(): pl.pallas_call(partial(attention_kernel, 4), out_shape=(jax.ShapeDtypeStr...  41.7 us
    pallas_call x1, Pallas kernels, finish(): pl.pallas_call(finish_kernel, out_shape=tuple((jax.ShapeDtypeStruct(shape...  40.4 us
    pallas_call x1, Pallas kernels, project(): pl.pallas_call(project_kernel, out_shape=(jax.ShapeDtypeStruct(counts.sha...  31.5 us
    pallas_call x1, Pallas kernels, emit(): pl.pallas_call(partial(emit_kernel, factor), grid=(2,), out_shape=tuple((...  3.85 us

profile of v10, /device:TPU:1, one launch (start us, length us, event | category | flops | bytes accessed | tf_op | source)
XLA Modules:
  0.0 118.2 jit_solution(7675755139379922747)
XLA Ops:
  0.6 31.5 %project.1 = (s32[1,32]{1,0:T(1,128)}, f32[1,128]{1,0:T(1,128)}, bf16[4096,512]{1,0:T(8,128)(2,1)}, bf16[4096,128]{1,0:T(8,128)(2,1)}, bf16[128,4096]{1,0:T(8,12...) custom-call(bf16[512,512]{1,0:T(8,128)(2,1)} %bitcast.12, bf16[512,512]{1,0:T(8,128)(2,1)} %bitcast.14, ...), custom_call_target="tpu_custom_call" | custom-call | tf_op jit(solution)/shard_map/project/pallas_call | solution.py:220
  32.2 41.7 %attention.1 = (bf16[256,4096]{1,0:T(8,128)(2,1)}, f32[192,512]{1,0:T(8,128)}) custom-call(s32[1,32]{1,0:T(1,128)} %get-tuple-element.21.order_ref, f32[1,128]{1,0:T(1,128)} %get-tuple-element.22.reach_ref, s32[8,32]{1,0:T(8,128)} %bitcast.17, s32[32]{0:T(128)} %bitcast.19, bf16[4096,128]{1,0:T(8,128)(2,1)} %get-tuple-element.23.kv_ref, ...), custom_call_target="tpu_custom_call" | custom-call | tf_op jit(solution)/shard_map/attention/pallas_call | solution.py:329
  73.9 40.4 %finish.1 = (bf16[512,512]{1,0:T(8,128)(2,1)}, bf16[512,512]{1,0:T(8,128)(2,1)}, bf16[512,512]{1,0:T(8,128)(2,1)}, bf16[512,1536]{1,0:T(8,128)(2,1)}) custom-call(bf16[4,64,4096]{2,1,0:T(8,128)(2,1)} %bitcast.11, f32[3,64,512]{2,1,0:T(8,128)} %bitcast.16, bf16[512,512]{1,0:T(8,128)(2,1)} %bitcast.13, bf16[512,512]{1,0:T(8,128)(2,1)} %bitcast.15, ...), custom_call_target="tpu_custom_call" | custom-call | tf_op jit(solution)/shard_map/finish/pallas_call | solution.py:597
  114.3 3.9 %emit.1 = (bf16[512,512]{1,0:T(8,128)(2,1)}, bf16[512,512]{1,0:T(8,128)(2,1)}, f32[512,512]{1,0:T(8,128)}, f32[512,1536]{1,0:T(8,128)}) custom-call(bf16[512,512]{1,0:T(8,128)(2,1)} %get-tuple-element.30.layer_ref, bf16[512,512]{1,0:T(8,128)(2,1)} %get-tuple-element.31.gradf_ref, bf16[512,512]{1,0:T(8,128)(2,1)} %get-tuple-element.32.osum_ref, ...), custom_call_target="tpu_custom_call" | custom-call | tf_op jit(solution)/shard_map/emit/pallas_call | solution.py:642
